TPU v7x, 128 devices: a whole 4x4x4 slice. The times are simulated.
128 devices in a mesh: lat: 2 (over z_lo), lon: 32 (over y, x, z_hi), tp: 2 (over core).
Axes of the slice: x: 4, y: 4, z: 4 (z_hi: 2, z_lo: 2; z = z_hi * 2 + z_lo), core: 2. Of those that a mesh axis runs over, the one named last changes fastest.
Arguments:
- tokens: bfloat16 [48, 768, 2, 1024], P('lat', 'lon', 'tp'), may hold values from -6 to 6
- land_mask: int32 [48, 768, 2], P('lat', 'lon', 'tp'), may hold values 0 or 1
- qkv_weight: bfloat16 [3, 1024, 1024], P(None, None, 'tp'), may hold values from -0.1875 to 0.1875
- out_weight: bfloat16 [1024, 1024], P('tp'), may hold values from -0.1875 to 0.1875
- out_grad: bfloat16 [48, 768, 2, 1024], P('lat', 'lon', 'tp'), may hold values from -6 to 6
Outputs:
- d_tokens: bfloat16 [48, 768, 2, 1024], P('lat', 'lon', 'tp')
- d_qkv_weight: float32 [3, 1024, 1024], P(None, 'lon', 'tp')
- d_out_weight: float32 [1024, 1024], P('tp', 'lon')
All inputs are finite; a program needn't handle non-finite values. No bound on the sum of `land_mask` on one device may be relied on, other than what follows from the above.
Results may differ from a plain program's by a relative error of at most 0.03.
The roundings to bfloat16 on the way count: a program that leaves them out, or rounds other values in their place, can miss the bound.
Values may be sent and summed in bfloat16 or wider, within the bound.
A program may use at most 128 MiB of HBM per device.

v0:
```python
import jax
import jax.numpy as jnp
from jax import lax
from jax.sharding import PartitionSpec as P

HEAD_DIM = 64
LEV = 2
WIN_LAT = 6
WIN_LON = 12
SHIFT_LAT = 3
SHIFT_LON = 6


def shifted(block, axis, distance):
    devices = range(lax.axis_size(axis))
    route = [((i - distance) % len(devices), i) for i in devices]
    return lax.ppermute(block, axis, route)


def shortened(array):
    return jax.tree.map(lambda a: a.astype(jnp.bfloat16) if a.dtype == jnp.float32 else a, array)


def window_split(grid):
    lat_rows, lon_cols = (grid.shape[0], grid.shape[1])
    tail = grid.shape[2:]
    grid = grid.reshape((lat_rows // WIN_LAT, WIN_LAT, lon_cols // WIN_LON, WIN_LON) + tail)
    grid = jnp.moveaxis(grid, 2, 1)
    return grid.reshape(
        (lat_rows // WIN_LAT * (lon_cols // WIN_LON), WIN_LAT * WIN_LON * tail[0]) + tail[1:]
    )


def window_merge(blocks, lat_rows, lon_cols):
    tail = blocks.shape[2:]
    blocks = blocks.reshape(
        (lat_rows // WIN_LAT, lon_cols // WIN_LON, WIN_LAT, WIN_LON, LEV) + tail
    )
    blocks = jnp.moveaxis(blocks, 2, 1)
    return blocks.reshape((lat_rows, lon_cols, LEV) + tail)


def window_grads(token_win, mask_win, region_win, grad_win, qkv_weight, out_weight):
    f32 = jnp.float32
    nwin, seq = (token_win.shape[0], token_win.shape[1])
    width = qkv_weight.shape[2]
    head_count = width // HEAD_DIM
    scale = HEAD_DIM ** (-0.5)
    features = token_win.astype(f32)
    mean_removed = features - jnp.mean(features, axis=-1, keepdims=True)
    variance = jnp.mean(mean_removed * mean_removed, axis=-1, keepdims=True)
    inverse_deviation = lax.rsqrt(variance + 1e-05)
    standardized_input = mean_removed * inverse_deviation
    normalized_tokens = standardized_input.astype(jnp.bfloat16)
    projected = jnp.einsum(
        "wsd,jde->jwse", normalized_tokens, qkv_weight, preferred_element_type=f32
    ).astype(jnp.bfloat16)
    heads = projected.reshape(3, nwin, seq, head_count, HEAD_DIM)
    queries, key_rows, value_rows = (heads[0], heads[1], heads[2])
    scores = jnp.einsum("wshe,wthe->whst", queries, key_rows, preferred_element_type=f32) * scale
    same_region = region_win[:, :, None] == region_win[:, None, :]
    diagonal = jnp.eye(seq, dtype=bool)[None]
    permitted_pairs = same_region & ((mask_win[:, None, :] == 1) | diagonal)
    scores = jnp.where(permitted_pairs[:, None], scores, -1e30)
    top_score = jnp.max(scores, axis=-1, keepdims=True)
    expo = jnp.exp(scores - top_score)
    prob_f32 = expo / jnp.sum(expo, axis=-1, keepdims=True)
    prob_bf16 = prob_f32.astype(jnp.bfloat16)
    attended = jnp.einsum(
        "whst,wthe->wshe", prob_bf16, value_rows, preferred_element_type=f32
    ).astype(jnp.bfloat16)
    attended = attended.reshape(nwin, seq, width)
    d_out_weight = jnp.einsum("wse,wsd->ed", attended, grad_win, preferred_element_type=f32)
    d_attended = jnp.einsum("wsd,ed->wse", grad_win, out_weight, preferred_element_type=f32).astype(
        jnp.bfloat16
    )
    d_attended = d_attended.reshape(nwin, seq, head_count, HEAD_DIM)
    d_prob = jnp.einsum("wshe,wthe->whst", d_attended, value_rows, preferred_element_type=f32)
    d_value = jnp.einsum(
        "whst,wshe->wthe", prob_bf16, d_attended, preferred_element_type=f32
    ).astype(jnp.bfloat16)
    d_scores = prob_f32 * (d_prob - jnp.sum(prob_f32 * d_prob, axis=-1, keepdims=True)) * scale
    d_scores = d_scores.astype(jnp.bfloat16)
    d_query = jnp.einsum("whst,wthe->wshe", d_scores, key_rows, preferred_element_type=f32).astype(
        jnp.bfloat16
    )
    d_key = jnp.einsum("whst,wshe->wthe", d_scores, queries, preferred_element_type=f32).astype(
        jnp.bfloat16
    )
    d_proj = jnp.stack([d_query, d_key, d_value]).reshape(3, nwin, seq, width)
    d_qkv_weight = jnp.einsum(
        "wsd,jwse->jde", normalized_tokens, d_proj, preferred_element_type=f32
    )
    normalized_gradient = jnp.einsum(
        "jwse,jde->wsd", d_proj, qkv_weight, preferred_element_type=f32
    )
    shifted_gradient = inverse_deviation * (
        normalized_gradient
        - jnp.mean(normalized_gradient, axis=-1, keepdims=True)
        - standardized_input
        * jnp.mean(normalized_gradient * standardized_input, axis=-1, keepdims=True)
    )
    return (shifted_gradient, d_qkv_weight, d_out_weight)


def body(tokens, land_mask, qkv_weight, out_weight, out_grad):
    rows_dev, cols_dev = (tokens.shape[0], tokens.shape[1])
    own_arrays = (tokens, land_mask, out_grad)
    upper_rims = shifted(
        (tokens[:SHIFT_LAT], land_mask[:SHIFT_LAT], out_grad[:SHIFT_LAT]), "lat", -1
    )
    rolled_rows = tuple(
        (
            jnp.concatenate([whole_part[SHIFT_LAT:], extra_part], axis=0)
            for whole_part, extra_part in zip(own_arrays, upper_rims)
        )
    )
    column_rims = shifted(
        (
            rolled_rows[0][:, :SHIFT_LON],
            shortened(rolled_rows[1][:, :SHIFT_LON]),
            rolled_rows[2][:, :SHIFT_LON],
        ),
        "lon",
        -1,
    )
    rolled_all = tuple(
        (
            jnp.concatenate([whole_part[:, SHIFT_LON:], extra_part], axis=1)
            for whole_part, extra_part in zip(rolled_rows, column_rims)
        )
    )
    full_tokens, full_mask, full_grad = (
        lax.all_gather(rolled_all[0], "tp", axis=2, tiled=True),
        lax.all_gather(shortened(rolled_all[1]), "tp", axis=2, tiled=True),
        lax.all_gather(rolled_all[2], "tp", axis=2, tiled=True),
    )
    lat_total = rows_dev * lax.axis_size("lat")
    row_ids = lax.axis_index("lat") * rows_dev + jnp.arange(rows_dev, dtype=jnp.int32)
    region_rows = ((row_ids + SHIFT_LAT) % lat_total < SHIFT_LAT).astype(jnp.int32)
    region_grid = jnp.broadcast_to(
        region_rows[:, None, None], (rows_dev, cols_dev, full_mask.shape[2])
    )
    shifted_gradient, d_qkv, d_out = window_grads(
        window_split(full_tokens),
        window_split(full_mask),
        window_split(region_grid),
        window_split(full_grad),
        qkv_weight,
        out_weight,
    )
    partial_grid = window_merge(shifted_gradient, rows_dev, cols_dev)
    shares = lax.psum_scatter(
        partial_grid.astype(jnp.bfloat16), "tp", scatter_dimension=2, tiled=True
    ).astype(jnp.float32)
    column_back = shifted(shares[:, cols_dev - SHIFT_LON :].astype(jnp.bfloat16), "lon", 1).astype(
        jnp.float32
    )
    shares = jnp.concatenate([column_back, shares[:, : cols_dev - SHIFT_LON]], axis=1)
    row_back = shifted(shares[rows_dev - SHIFT_LAT :].astype(jnp.bfloat16), "lat", 1).astype(
        jnp.float32
    )
    shares = jnp.concatenate([row_back, shares[: rows_dev - SHIFT_LAT]], axis=0)
    d_tokens = (shares + out_grad.astype(jnp.float32)).astype(jnp.bfloat16)
    sector_part = (
        lax.psum_scatter(d_qkv.astype(jnp.bfloat16), "lon", scatter_dimension=1, tiled=True).astype(
            jnp.float32
        ),
        lax.psum_scatter(d_out.astype(jnp.bfloat16), "lon", scatter_dimension=1, tiled=True).astype(
            jnp.float32
        ),
    )
    d_qkv_weight, d_out_weight = (
        lax.psum(sector_part[0].astype(jnp.bfloat16), "lat").astype(jnp.float32),
        lax.psum(sector_part[1].astype(jnp.bfloat16), "lat").astype(jnp.float32),
    )
    return (d_tokens, d_qkv_weight, d_out_weight)


def solution(mesh):
    in_specs = (
        P("lat", "lon", "tp", None),
        P("lat", "lon", "tp"),
        P(None, None, "tp"),
        P("tp", None),
        P("lat", "lon", "tp", None),
    )
    out_specs = (P("lat", "lon", "tp", None), P(None, "lon", "tp"), P("tp", "lon"))
    return jax.shard_map(body, mesh=mesh, in_specs=in_specs, out_specs=out_specs, check_vma=False)
```

profile of v0, /device:TPU:0, one launch (start us, length us, event | category | flops | bytes accessed | tf_op | source)
XLA Modules:
  0.0 850.0 jit_solution(12478335235526027775)
XLA Ops:
  14.3 8.4 collective-permute-start.1
  23.0 7.2 collective-permute-done.1
  39.7 8.2 collective-permute-start.3
  53.1 8.1 collective-permute-start.5
  63.5 6.4 collective-permute-done.5
  71.4 4.1 copy.100
  77.7 4.0 copy.106
  81.7 4.1 reduce_sum.54
  85.9 5.0 multiply_reduce_fusion.1
  93.1 7.1 reshape.128
  100.2 6.5 convert_bitcast_fusion
  119.3 4.1 copy.117
  126.9 6.1 reshape.125
  133.0 4.4 convolution_convert_fusion
  137.4 3.9 copy.156
  141.3 7.4 fusion.66
  148.7 9.5 %fusion.65 = (f32[8,8,144]{2,1,0:T(8,128)S(1)}, f32[8,8,144,144]{2,3,1,0:T(8,128)}) fusion(pred[8,144,144]{1,2,0:T(8,128)(4,1)S(1)} %copy-done.4, bf16[8,144,8,64]{1,3,2,0:T(8,128)(2,1)} %bitcast.105, bf16[8,144,8,64]{1,3,2,0:T(8,128)(2,1)} %bitcast.103), kind=kOutput, calls=%fused_computation.83 | convolution fusion | flops 175177872 | bytes 7870464 | tf_op jit(solution)/shard_map/sub | solution.py:66
  158.2 16.9 %fusion.38 = bf16[8,8,64,144]{3,2,1,0:T(8,128)(2,1)} fusion(bf16[8,144,8,64]{1,3,2,0:T(8,128)(2,1)} %bitcast.104, f32[8,8,144,144]{2,3,1,0:T(8,128)} %fusion.66, f32[8,8,144,144]{2,3,1,0:T(8,128)} %get-tuple-element.21, f32[8,8,144]{2,1,0:T(8,128)S(1)} %get-tuple-element.20), kind=kOutput, calls=%fused_computation.41 | convolution fusion | flops 179758224 | bytes 13012992 | tf_op jit(solution)/shard_map/whst,wthe->wshe/dot_general | solution.py:84
  175.1 16.9 %fusion.41 = bf16[8,8,64,144]{3,2,1,0:T(8,128)(2,1)} fusion(bf16[8,144,8,64]{1,3,2,0:T(8,128)(2,1)} %bitcast.106, f32[8,8,144,144]{2,3,1,0:T(8,128)} %fusion.66, f32[8,8,144,144]{2,3,1,0:T(8,128)} %get-tuple-element.21, f32[8,8,144]{2,1,0:T(8,128)S(1)} %get-tuple-element.20), kind=kOutput, calls=%fused_computation.42 | convolution fusion | flops 179758224 | bytes 13012992 | tf_op jit(solution)/shard_map/whst,wshe->wthe/dot_general | solution.py:87
  192.0 7.4 fusion.32
  210.5 6.9 bitcast_reduce_fusion
  217.5 4.0 fusion.8
  221.5 5.9 convert_element_type.128
  227.4 3.9 copy.130
  233.6 9.5 %fusion.20 = bf16[3,1024,512]{1,2,0:T(8,128)(2,1)} fusion(bf16[1,8,144,512]{3,2,0,1:T(8,128)(2,1)} %copy.129, bf16[1,8,144,512]{3,2,0,1:T(8,128)(2,1)} %copy.128, bf16[1,8,144,512]{3,2,0,1:T(8,128)(2,1)} %copy.127, f32[8,144,1024]{2,1,0:T(8,128)} %reshape.128, f32[8,144]{1,0:T(8,128)S(1)} %reshape.138, f32[8,144]{1,0:T(8,128)S(1)} %reshape.137), kind=kOutput, calls=%fused_computation.27 | convolution fusion | flops 3632529408 | bytes 11412480 | tf_op jit(solution)/shard_map/wsd,jwse->jde/dot_general | solution.py:91
  243.1 7.8 copy.135
  251.2 5.3 fusion.35
  262.6 16.0 %collective-permute-done.6 = bf16[24,6,1,1024]{3,0,2,1:T(8,128)(2,1)} collective-permute-done((bf16[24,6,1,1024]{3,0,2,1:T(8,128)(2,1)S(1)}, bf16[24,6,1,1024]{3,0,2,1:T(8,128)(2,1)}, u32[]{:S(2)}, u32[]{:S(2)}) %collective-permute-start.6) | collective-permute-done | bytes 294944 | tf_op jit(solution)/shard_map/ppermute | solution.py:17
  282.0 342.0 %all-reduce.6.cloned.1.call-done = bf16[3,1024,512]{2,0,1:T(4,128)(2,1)} async-done(((bf16[3,1024,512]{2,0,1:T(4,128)(2,1)}), bf16[3,1024,512]{2,0,1:T(4,128)(2,1)}) %all-reduce.6.cloned.1.call-update) | async-done | bytes 3145744
  625.6 186.9 %reduce-scatter.5.cloned.1.call-done = bf16[512,32]{0,1:T(8,128)(2,1)} async-done(((bf16[512,1024]{0,1:T(8,128)(2,1)}), bf16[512,32]{0,1:T(8,128)(2,1)}) %reduce-scatter.5.cloned.1.call-update) | async-done | bytes 32784 | tf_op jit(solution)/shard_map/reduce_scatter | solution.py:169
  812.6 8.8 %psum.15 = bf16[512,32]{0,1:T(8,128)(2,1)} all-reduce(bf16[512,32]{0,1:T(8,128)(2,1)} %reduce-scatter.5.cloned.1.call-done), channel_id=1, replica_groups=mesh['lat'=2,'lon'=32,'tp'=2] {'lat'}, use_global_device_ids=true, to_apply=%region_11.12 | all-reduce | flops 16384 | bytes 65536 | tf_op jit(solution)/shard_map/psum | solution.py:175
  822.8 15.3 %all-reduce.4.cloned.1.call-done = bf16[3,32,512]{2,0,1:T(4,128)(2,1)} async-done(((bf16[3,32,512]{2,0,1:T(4,128)(2,1)}), bf16[3,32,512]{2,0,1:T(4,128)(2,1)}) %all-reduce.4.cloned.1.call-update) | async-done | bytes 98320 | tf_op jit(solution)/shard_map/psum | solution.py:174
  (91 shorter events, 76.5 us)
Async XLA Ops:
  7.2 93.1 %copy-start = (bf16[3,1024,512]{2,1,0:T(8,128)(2,1)S(1)}, bf16[3,1024,512]{2,1,0:T(8,128)(2,1)}, u32[]{:S(2)}) copy-start(bf16[3,1024,512]{2,1,0:T(8,128)(2,1)} %param.7) | copy-start | bytes 9437188
  7.2 64.2 %all-gather.3.cloned.1.call-start = ((), (), s32[]{:S(2)}) async-start(), calls=%async_computation.2 | async-start | bytes 3538944 | tf_op jit(solution)/shard_map/all_gather | solution.py:134
  8.3 5.9 collective-permute-start
  14.3 15.9 %collective-permute-start.1 = (bf16[24,6,1,1024]{3,1,2,0:T(8,128)(2,1)S(1)}, bf16[24,6,1,1024]{3,1,2,0:T(8,128)(2,1)S(1)}, u32[]{:S(2)}, u32[]{:S(2)}) collective-permute-start(bf16[24,6,1,1024]{3,1,2,0:T(8,128)(2,1)S(1)} %pad_maximum_fusion.7), channel_id=1, source_target_pairs={{2,0},{4,2},{6,4},{8,6},{10,8},{12,10},{14,12},{16,14},{18,16},{20... | collective-permute-start | bytes 884744 | tf_op jit(solution)/shard_map/ppermute | solution.py:17
  23.0 8.5 %copy-start.5 = (s32[24,24,1]{1,2,0:T(1,128)S(1)}, s32[24,24,1]{1,2,0:T(1,128)}, u32[]{:S(2)}) copy-start(s32[24,24,1]{1,2,0:T(1,128)} %param.6) | copy-start | bytes 6916
  31.5 87.9 %all-gather.5.cloned.1.call-start = ((), (), s32[]{:S(2)}) async-start(), calls=%async_computation.3 | async-start | bytes 3538944 | tf_op jit(solution)/shard_map/all_gather | solution.py:136
  32.1 6.9 collective-permute-start.2
  34.7 17.2 %collective-permute-start.4 = (bf16[3,24,1,1024]{3,1,2,0:T(8,128)(2,1)}, bf16[3,24,1,1024]{3,1,2,0:T(8,128)(2,1)}, u32[]{:S(2)}, u32[]{:S(2)}) collective-permute-start(bf16[3,24,1,1024]{3,1,2,0:T(8,128)(2,1)} %slice.75), channel_id=1, source_target_pairs={{64,0},{0,64},{65,1},{1,65},{66,2},{2,66},{67,3},{3,67},{68,4},{4,... | collective-permute-start | bytes 442376 | tf_op jit(solution)/shard_map/ppermute | solution.py:17
  39.7 9.6 %collective-permute-start.3 = (s32[24,6,1]{1,0,2:T(8,128)S(1)}, s32[24,6,1]{1,0,2:T(8,128)S(1)}, u32[]{:S(2)}, u32[]{:S(2)}) collective-permute-start(s32[24,6,1]{1,0,2:T(8,128)S(1)} %pad_add_fusion), channel_id=1, source_target_pairs={{2,0},{4,2},{6,4},{8,6},{10,8},{12,10},{14,12},{16,14},{18,16},{20... | collective-permute-start | bytes 1736 | tf_op jit(solution)/shard_map/ppermute | solution.py:17
  51.9 10.3 %copy-start.2 = (bf16[21,24,1,1024]{3,1,2,0:T(8,128)(2,1)S(1)}, bf16[21,24,1,1024]{3,1,2,0:T(8,128)(2,1)}, u32[]{:S(2)}) copy-start(bf16[21,24,1,1024]{3,1,2,0:T(8,128)(2,1)} %slice.74) | copy-start | bytes 3096580
  53.1 16.8 %collective-permute-start.5 = (bf16[24,6,1,1024]{3,1,2,0:T(8,128)(2,1)S(1)}, bf16[24,6,1,1024]{3,1,2,0:T(8,128)(2,1)S(1)}, u32[]{:S(2)}, u32[]{:S(2)}) collective-permute-start(bf16[24,6,1,1024]{3,1,2,0:T(8,128)(2,1)S(1)} %pad_maximum_fusion.6), channel_id=1, source_target_pairs={{2,0},{4,2},{6,4},{8,6},{10,8},{12,10},{14,12},{16,14},{18,16},{20... | collective-permute-start | bytes 884744 | tf_op jit(solution)/shard_map/ppermute | solution.py:17
  71.1 188.9 %reduce-scatter.3.cloned.1.call-start = ((), (), s32[]{:S(2)}) async-start(), calls=%async_computation.4 | async-start | bytes 3538944 | tf_op jit(solution)/shard_map/reduce_scatter | solution.py:153
  75.5 2.2 copy-start.1
  141.3 7.4 copy-start.4
  233.5 390.5 %all-reduce.6.cloned.1.call-start = ((), (), s32[]{:S(2)}) async-start(), calls=%async_computation.7 | async-start | bytes 8388608
  250.9 561.7 %reduce-scatter.5.cloned.1.call-start = ((), (), s32[]{:S(2)}) async-start(), calls=%async_computation.6 | async-start | bytes 1081344 | tf_op jit(solution)/shard_map/reduce_scatter | solution.py:169
  251.2 5.3 copy-start.3
  259.9 1.5 copy-start.6
  259.9 578.1 %all-reduce.4.cloned.1.call-start = ((), (), s32[]{:S(2)}) async-start(), calls=%async_computation.5 | async-start | bytes 262144 | tf_op jit(solution)/shard_map/psum | solution.py:174
  261.3 17.3 %collective-permute-start.6 = (bf16[24,6,1,1024]{3,0,2,1:T(8,128)(2,1)S(1)}, bf16[24,6,1,1024]{3,0,2,1:T(8,128)(2,1)}, u32[]{:S(2)}, u32[]{:S(2)}) collective-permute-start(bf16[24,6,1,1024]{3,0,2,1:T(8,128)(2,1)S(1)} %copy.132), channel_id=1, source_target_pairs={{62,0},{0,2},{2,4},{4,6},{6,8},{8,10},{10,12},{12,14},{14,16},{16,... | collective-permute-start | bytes 884744 | tf_op jit(solution)/shard_map/ppermute | solution.py:17
  281.4 558.3 %collective-permute-start.7 = (bf16[3,24,1,1024]{3,1,0,2:T(8,128)(2,1)}, bf16[3,24,1,1024]{3,1,0,2:T(8,128)(2,1)}, u32[]{:S(2)}, u32[]{:S(2)}) collective-permute-start(bf16[3,24,1,1024]{3,1,0,2:T(8,128)(2,1)} %pad_maximum_fusion.8), channel_id=1, source_target_pairs={{64,0},{0,64},{65,1},{1,65},{66,2},{2,66},{67,3},{3,67},{68,4},{4,... | collective-permute-start | bytes 442376 | tf_op jit(solution)/shard_map/ppermute | solution.py:17
Sparse Core Ops, SparseCore 0:
  31.6 15.2 all-gather.2
  71.3 15.2 all-gather.4
  233.6 14.2 reduce-scatter.2
  251.0 372.9 all-reduce.5
  626.9 185.6 reduce-scatter.4
  815.4 22.6 all-reduce.3
where the time goes:
time: 856 us; the launch traced here: 850 us
  waiting for transfers between devices  577 us (67%)
  local copies, waits for them, and re-layouts  95.3 us (11%)
  matrix products  94.1 us (11%)
  starting transfers between devices  30.2 us (4%)
  other arithmetic  27.5 us (3%)
  between operations  15.3 us (2%)
  blocking collectives  10.6 us (1%)
    unnamed x7, waiting for transfers between devices  342 us
    reduce_scatter x1, waiting for transfers between devices, body(): lax.psum_scatter(d_out.astype(jnp.bfloat16), 'lon', scatter_dimension=1,...  187 us
    ppermute x8, waiting for transfers between devices, shifted(): return lax.ppermute(block, axis, route)  32.8 us
    ppermute x8, starting transfers between devices, shifted(): return lax.ppermute(block, axis, route)  29.5 us
  transfers between devices with their start and end apart: 14, of which 8 were waited for; matrix products, arithmetic and copies ran while one was open for 11% of the time, Pallas kernels for 0%

commit v1 on v0

--- a/solution.py
+++ b/solution.py
@@ -1,6 +1,8 @@
 import jax
 import jax.numpy as jnp
 from jax import lax
+from jax.experimental import pallas as pl
+from jax.experimental.pallas import tpu as pltpu
 from jax.sharding import PartitionSpec as P
 
 HEAD_DIM = 64
@@ -70,7 +72,7 @@
         "whst,wthe->wshe", prob_bf16, value_rows, preferred_element_type=f32
     ).astype(jnp.bfloat16)
     attended = attended.reshape(nwin, seq, width)
-    d_out_weight = jnp.einsum("wse,wsd->ed", attended, grad_win, preferred_element_type=f32)
+    d_out_weight = jnp.einsum("wse,wsd->de", attended, grad_win, preferred_element_type=f32)
     d_attended = jnp.einsum("wsd,ed->wse", grad_win, out_weight, preferred_element_type=f32).astype(
         jnp.bfloat16
     )
@@ -103,6 +105,141 @@
     return (shifted_gradient, d_qkv_weight, d_out_weight)
 
 
+def place():
+    lat, lon, tp = (lax.axis_index(a) for a in ("lat", "lon", "tp"))
+    return lon // 8, (lon // 2) % 4, (lon % 2) * 2 + lat, tp
+
+
+def device_at(y, x, z, tp):
+    return (z % 2, (y * 4 + x) * 2 + z // 2, tp)
+
+
+def reduce_peers():
+    y, x, z, tp = place()
+    along_y = [device_at((y + d) % 4, x, z, tp) for d in (1, 2, 3)]
+    along_x = [device_at(y, (x + d) % 4, z, tp) for d in (1, 2, 3)]
+    along_z = [device_at(y, x, (z + d) % 4, tp) for d in (1, 2, 3)]
+    return along_y, along_x, along_z
+
+
+def reduce_kernel(grads, out, got1, mid1, got2, mid2, got3, send_sem, recv_sem):
+    y, x, z, tp = place()
+    along_y, along_x, along_z = reduce_peers()
+    barrier = pltpu.get_barrier_semaphore()
+    for peer in along_y + along_x + along_z:
+        pl.semaphore_signal(barrier, inc=1, device_id=peer, device_id_type=pl.DeviceIdType.MESH)
+    pl.semaphore_wait(barrier, 9)
+
+    def copy(src, dst, color, stage, slot, peer):
+        return pltpu.make_async_remote_copy(
+            src_ref=src,
+            dst_ref=dst,
+            send_sem=send_sem.at[color, stage, slot],
+            recv_sem=recv_sem.at[color, stage, slot],
+            device_id=peer,
+            device_id_type=pl.DeviceIdType.MESH,
+        )
+
+    first, second = ((y, x), (x, y))
+    peers = ((along_y, along_x), (along_x, along_y))
+    copies1 = []
+    for color in (0, 1):
+        copies1.append(
+            [
+                copy(
+                    grads.at[color, :, (first[color] + d) % 4],
+                    got1.at[color, d - 1],
+                    color, 0, d - 1, peers[color][0][d - 1],
+                )
+                for d in (1, 2, 3)
+            ]
+        )
+        for c in copies1[color]:
+            c.start()
+    copies2 = []
+    for color in (0, 1):
+        for c in copies1[color]:
+            c.wait_recv()
+        for m in range(2):
+            for b in range(4):
+                total = grads[color, m, first[color], b].astype(jnp.float32)
+                for d in range(3):
+                    total += got1[color, d, m, b].astype(jnp.float32)
+                mid1[color, m, b] = total.astype(jnp.bfloat16)
+        copies2.append(
+            [
+                copy(
+                    mid1.at[color, :, (second[color] + d) % 4],
+                    got2.at[color, d - 1],
+                    color, 1, d - 1, peers[color][1][d - 1],
+                )
+                for d in (1, 2, 3)
+            ]
+        )
+        for c in copies2[color]:
+            c.start()
+    copies3 = []
+    for color in (0, 1):
+        for c in copies2[color]:
+            c.wait_recv()
+        for m in range(2):
+            total = mid1[color, m, second[color]].astype(jnp.float32)
+            for d in range(3):
+                total += got2[color, d, m].astype(jnp.float32)
+            total = total.astype(jnp.bfloat16)
+            mid2[color, 0, m] = total[:32]
+            mid2[color, 1, m] = total[32:]
+        for m in range(2):
+            got3[z, color, m] = mid2[color, z // 2, m]
+        copies3.append(
+            [
+                copy(
+                    mid2.at[color, ((z + d) % 4) // 2],
+                    got3.at[z, color],
+                    color, 2, d - 1, along_z[d - 1],
+                )
+                for d in (1, 2, 3)
+            ]
+        )
+        for c in copies3[color]:
+            c.start()
+    for color in (0, 1):
+        for c in copies3[color]:
+            c.wait_recv()
+        for m in range(2):
+            total = got3[0, color, m].astype(jnp.float32)
+            for i in range(1, 4):
+                total += got3[i, color, m].astype(jnp.float32)
+            out[2 * color + m] = total
+    for group in copies1 + copies2 + copies3:
+        for c in group:
+            c.wait_send()
+
+
+def reduce_weights(grads):
+    cols = grads.shape[-1]
+    bf16 = jnp.bfloat16
+    return pl.pallas_call(
+        reduce_kernel,
+        out_shape=jax.ShapeDtypeStruct((4, 32, cols), jnp.float32),
+        in_specs=[pl.BlockSpec(memory_space=pltpu.VMEM)],
+        out_specs=pl.BlockSpec(memory_space=pltpu.VMEM),
+        scratch_shapes=[
+            pltpu.VMEM((2, 3, 2, 4, 64, cols), bf16),
+            pltpu.VMEM((2, 2, 4, 64, cols), bf16),
+            pltpu.VMEM((2, 3, 2, 64, cols), bf16),
+            pltpu.VMEM((2, 2, 2, 32, cols), bf16),
+            pltpu.VMEM((4, 2, 2, 32, cols), bf16),
+            pltpu.SemaphoreType.DMA((2, 3, 3)),
+            pltpu.SemaphoreType.DMA((2, 3, 3)),
+        ],
+        compiler_params=pltpu.CompilerParams(
+            collective_id=0, has_side_effects=True, vmem_limit_bytes=48 * 1024 * 1024
+        ),
+        name="reduce_weights",
+    )(grads)
+
+
 def body(tokens, land_mask, qkv_weight, out_weight, out_grad):
     rows_dev, cols_dev = (tokens.shape[0], tokens.shape[1])
     own_arrays = (tokens, land_mask, out_grad)
@@ -162,18 +299,12 @@
     )
     shares = jnp.concatenate([row_back, shares[: rows_dev - SHIFT_LAT]], axis=0)
     d_tokens = (shares + out_grad.astype(jnp.float32)).astype(jnp.bfloat16)
-    sector_part = (
-        lax.psum_scatter(d_qkv.astype(jnp.bfloat16), "lon", scatter_dimension=1, tiled=True).astype(
-            jnp.float32
-        ),
-        lax.psum_scatter(d_out.astype(jnp.bfloat16), "lon", scatter_dimension=1, tiled=True).astype(
-            jnp.float32
-        ),
-    )
-    d_qkv_weight, d_out_weight = (
-        lax.psum(sector_part[0].astype(jnp.bfloat16), "lat").astype(jnp.float32),
-        lax.psum(sector_part[1].astype(jnp.bfloat16), "lat").astype(jnp.float32),
-    )
+    width = d_out.shape[1]
+    blocks = jnp.concatenate([d_qkv, d_out[None]]).astype(jnp.bfloat16)
+    blocks = blocks.reshape(2, 2, 4, 4, 64, width)
+    blocks = jnp.stack([blocks[0], jnp.swapaxes(blocks[1], 1, 2)])
+    reduced = reduce_weights(blocks)
+    d_qkv_weight, d_out_weight = reduced[:3], reduced[3].T
     return (d_tokens, d_qkv_weight, d_out_weight)
 
 

time: 856 us -> 337 us (0.39)
  waiting for transfers between devices: 577 us -> 21.2 us
  Pallas kernels: 0 us -> 44.1 us
  blocking collectives: 10.6 us -> 1.81 us
    unnamed x7 -> x3, waiting for transfers between devices: 342 us -> 0.05 us
    reduce_scatter x1 -> x0, waiting for transfers between devices: 187 us -> none  [body(): lax.psum_scatter(d_out.astype(jnp.bfloat16), 'lon', scatter_dimension=1,...]
    pallas_call x0 -> x1, Pallas kernels: none -> 44.1 us  [reduce_weights(): pl.pallas_call(reduce_kernel, out_shape=jax.ShapeDtypeStruct((4, 32, cols...]
    psum x1 -> x0, waiting for transfers between devices: 15.3 us -> none  [body(): lax.psum(sector_part[0].astype(jnp.bfloat16), 'lat').astype(jnp.float32)]
    ppermute x8, waiting for transfers between devices: 32.8 us -> 21.1 us  [shifted(): return lax.ppermute(block, axis, route)]
    slice x0 -> x3, local copies, waits for them, and re-layouts: none -> 8.82 us  [the longest x2 8.12 us: body(): blocks = jnp.stack([blocks[0], jnp.swapaxes(blocks[1], 1, 2)])]
    psum x1 -> x0, blocking collectives: 8.79 us -> none  [body(): lax.psum(sector_part[1].astype(jnp.bfloat16), 'lat').astype(jnp.float32)]
  transfers between devices with their start and end apart: 14 -> 11, of which waited for: 8 -> 5; matrix products, arithmetic and copies ran while one was open for 11% -> 29% of each run, Pallas kernels for 0% -> 13%
where the time goes in v1:
time: 337 us; the launch traced here: 331 us
  local copies, waits for them, and re-layouts  96.4 us (29%)
  matrix products  92.5 us (27%)
  Pallas kernels  44.1 us (13%)
  starting transfers between devices  30.7 us (9%)
  other arithmetic  30 us (9%)
  waiting for transfers between devices  21.2 us (6%)
  between operations  14.3 us (4%)
    pallas_call x1, Pallas kernels, reduce_weights(): pl.pallas_call(reduce_kernel, out_shape=jax.ShapeDtypeStruct((4, 32, cols...  44.1 us
    ppermute x8, starting transfers between devices, shifted(): return lax.ppermute(block, axis, route)  30.4 us
    ppermute x8, waiting for transfers between devices, shifted(): return lax.ppermute(block, axis, route)  21.1 us
    dot_general x1, matrix products, window_grads(): jnp.einsum('whst,wshe->wthe', d_scores, queries, preferred_element_type=f32)  17.1 us
    dot_general x1, matrix products, window_grads(): jnp.einsum('whst,wthe->wshe', d_scores, key_rows, preferred_element_type=...  17 us
    convert_element_type x3, local copies, waits for them, and re-layouts, window_grads(): features = token_win.astype(f32)  15.3 us
    convert_element_type x3, local copies, waits for them, and re-layouts, body(): partial_grid.astype(jnp.bfloat16)  11.9 us
    another operation x3, local copies, waits for them, and re-layouts, window_grads(): d_proj = jnp.stack([d_query, d_key, d_value]).reshape(3, nwin, seq, width)  11.2 us
  transfers between devices with their start and end apart: 11, of which 5 were waited for; matrix products, arithmetic and copies ran while one was open for 29% of the time, Pallas kernels for 13%

profile of v1, /device:TPU:0, one launch (start us, length us, event | category | flops | bytes accessed | tf_op | source)
XLA Modules:
  0.0 331.0 jit_solution(1128492981697299796)
XLA Ops:
  14.3 8.4 %collective-permute-start.1 = (bf16[24,6,1,1024]{3,1,2,0:T(8,128)(2,1)S(1)}, bf16[24,6,1,1024]{3,1,2,0:T(8,128)(2,1)S(1)}, u32[]{:S(2)}, u32[]{:S(2)}) collective-permute-start(bf16[24,6,1,1024]{3,1,2,0:T(8,128)(2,1)S(1)} %pad_maximum_fusion.9), channel_id=1, source_target_pairs={{2,0},{4,2},{6,4},{8,6},{10,8},{12,10},{14,12},{16,14},{18,16},{20... | collective-permute-start | bytes 884744 | tf_op jit(solution)/shard_map/ppermute | solution.py:19
  23.0 7.2 %collective-permute-done.1 = bf16[24,6,1,1024]{3,1,2,0:T(8,128)(2,1)S(1)} collective-permute-done((bf16[24,6,1,1024]{3,1,2,0:T(8,128)(2,1)S(1)}, bf16[24,6,1,1024]{3,1,2,0:T(8,128)(2,1)S(1)}, u32[]{:S(2)}, u32[]{:S(2)}) %collective-permute-start.1) | collective-permute-done | bytes 294944 | tf_op jit(solution)/shard_map/ppermute | solution.py:19
  39.7 8.2 %collective-permute-start.3 = (s32[24,6,1]{1,0,2:T(8,128)S(1)}, s32[24,6,1]{1,0,2:T(8,128)S(1)}, u32[]{:S(2)}, u32[]{:S(2)}) collective-permute-start(s32[24,6,1]{1,0,2:T(8,128)S(1)} %pad_add_fusion), channel_id=1, source_target_pairs={{2,0},{4,2},{6,4},{8,6},{10,8},{12,10},{14,12},{16,14},{18,16},{20... | collective-permute-start | bytes 1736 | tf_op jit(solution)/shard_map/ppermute | solution.py:19
  53.1 8.1 %collective-permute-start.5 = (bf16[24,6,1,1024]{3,1,2,0:T(8,128)(2,1)S(1)}, bf16[24,6,1,1024]{3,1,2,0:T(8,128)(2,1)S(1)}, u32[]{:S(2)}, u32[]{:S(2)}) collective-permute-start(bf16[24,6,1,1024]{3,1,2,0:T(8,128)(2,1)S(1)} %pad_maximum_fusion.8), channel_id=1, source_target_pairs={{2,0},{4,2},{6,4},{8,6},{10,8},{12,10},{14,12},{16,14},{18,16},{20... | collective-permute-start | bytes 884744 | tf_op jit(solution)/shard_map/ppermute | solution.py:19
  63.5 6.4 %collective-permute-done.5 = bf16[24,6,1,1024]{3,1,2,0:T(8,128)(2,1)S(1)} collective-permute-done((bf16[24,6,1,1024]{3,1,2,0:T(8,128)(2,1)S(1)}, bf16[24,6,1,1024]{3,1,2,0:T(8,128)(2,1)S(1)}, u32[]{:S(2)}, u32[]{:S(2)}) %collective-permute-start.5) | collective-permute-done | bytes 294944 | tf_op jit(solution)/shard_map/ppermute | solution.py:19
  71.4 4.1 %copy.106 = f32[24,24,2,1024]{3,2,1,0:T(2,128)S(1)} copy(bf16[24,24,2,1024]{3,1,2,0:T(8,128)(2,1)} %all-gather.3.cloned.1.call-done) | data formatting | bytes 7077888 | tf_op jit(solution)/shard_map/convert_element_type | solution.py:51
  77.7 4.0 %copy.112 = f32[4,2,6,12,2,1024]{5,4,3,2,1,0:T(2,128)} copy(f32[4,2,6,12,2,1024]{5,4,3,1,2,0:T(2,128)S(1)} %bitcast.106) | data formatting | bytes 9437184 | tf_op jit(solution)/shard_map/convert_element_type | solution.py:51
  81.7 4.1 %reduce_sum.54 = f32[4,2,6,12,2]{4,3,1,2,0:T(8,128)S(1)} reduce(f32[4,2,6,12,2,1024]{5,4,3,1,2,0:T(2,128)} %bitcast.107, f32[]{:T(128)} %constant.14.clone.1), dimensions={5}, to_apply=%region_0.1 | reduce | flops 1178496 | bytes 4723204 | tf_op jit(solution)/shard_map/reduce_sum | solution.py:52
  85.9 5.0 %multiply_reduce_fusion.1 = f32[4,2,6,12,2]{4,3,1,2,0:T(8,128)S(1)} fusion(f32[4,2,6,12,2,1024]{5,4,3,1,2,0:T(2,128)} %bitcast.108, f32[4,2,6,12,2]{4,3,1,2,0:T(8,128)S(1)} %broadcast_multiply_fusion), kind=kLoop, calls=%fused_computation.22 | loop fusion | flops 3537792 | bytes 4727808 | tf_op jit(solution)/shard_map/reduce_sum | solution.py:53
  93.1 7.2 %reshape.132 = f32[8,144,1024]{2,1,0:T(8,128)} reshape(f32[4,2,6,12,2,1024]{5,4,3,2,1,0:T(2,128)} %copy.112) | data formatting | bytes 9437184 | tf_op jit(solution)/shard_map/convert_element_type | solution.py:51
  100.3 6.5 %convert_bitcast_fusion = bf16[3,8,144,512]{3,2,0,1:T(8,128)(2,1)S(1)} fusion(bf16[3,1024,512]{2,1,0:T(8,128)(2,1)S(1)} %copy-done, f32[8,144,1024]{2,1,0:T(8,128)} %reshape.132, f32[8,144]{1,0:T(8,128)S(1)} %reshape.142, f32[8,144]{1,0:T(8,128)S(1)} %reshape.141), kind=kOutput, calls=%fused_computation.27 | convolution fusion | flops 3629187072 | bytes 11412480 | tf_op jit(solution)/shard_map/wsd,jde->jwse/dot_general | solution.py:57
  119.4 4.1 %copy.123 = bf16[24,24,2,1024]{3,2,1,0:T(2,128)(2,1)S(1)} copy(bf16[24,24,2,1024]{3,1,2,0:T(8,128)(2,1)} %all-gather.5.cloned.1.call-done) | data formatting | bytes 4718592 | tf_op jit(solution)/shard_map/all_gather | solution.py:273
  126.9 6.1 %reshape.129 = bf16[8,144,1024]{2,1,0:T(8,128)(2,1)} reshape(bf16[4,2,6,12,2,1024]{5,4,3,2,1,0:T(2,128)(2,1)} %copy.124) | data formatting | bytes 4718592 | tf_op jit(solution)/shard_map/reshape | solution.py:31
  133.0 4.4 %convolution_convert_fusion = bf16[8,144,512]{2,1,0:T(8,128)(2,1)} fusion(bf16[8,144,1024]{2,1,0:T(8,128)(2,1)} %reshape.129, bf16[512,1024]{1,0:T(8,128)(2,1)} %param.8), kind=kOutput, calls=%fused_computation.46 | convolution fusion | flops 1208549376 | bytes 4587520 | tf_op jit(solution)/shard_map/wsd,ed->wse/dot_general | solution.py:76
  137.4 4.0 %copy.166 = bf16[8,144,512]{1,2,0:T(8,128)(2,1)} copy(bf16[8,144,512]{2,1,0:T(8,128)(2,1)} %convolution_convert_fusion) | data formatting | bytes 2359296 | tf_op jit(solution)/shard_map/reshape | solution.py:79
  141.4 7.4 %fusion.68 = f32[8,8,144,144]{2,3,1,0:T(8,128)} fusion(bf16[8,144,8,64]{1,3,2,0:T(8,128)(2,1)} %bitcast.114, bf16[8,144,8,64]{1,3,2,0:T(8,128)(2,1)} %bitcast.112), kind=kOutput, calls=%fused_computation.89 | convolution fusion | flops 169869312 | bytes 7667712 | tf_op jit(solution)/shard_map/wshe,wthe->whst/dot_general | solution.py:80
  148.8 9.5 %fusion.67 = (f32[8,8,144]{2,1,0:T(8,128)S(1)}, f32[8,8,144,144]{2,3,1,0:T(8,128)}) fusion(pred[8,144,144]{1,2,0:T(8,128)(4,1)S(1)} %copy-done.9, bf16[8,144,8,64]{1,3,2,0:T(8,128)(2,1)} %bitcast.122, bf16[8,144,8,64]{1,3,2,0:T(8,128)(2,1)} %bitcast.120), kind=kOutput, calls=%fused_computation.88 | convolution fusion | flops 175177872 | bytes 7870464 | tf_op jit(solution)/shard_map/sub | solution.py:68
  158.3 17.0 %fusion.38 = bf16[8,8,64,144]{3,2,1,0:T(8,128)(2,1)} fusion(bf16[8,144,8,64]{1,3,2,0:T(8,128)(2,1)} %bitcast.121, f32[8,8,144,144]{2,3,1,0:T(8,128)} %fusion.68, f32[8,8,144,144]{2,3,1,0:T(8,128)} %get-tuple-element.20, f32[8,8,144]{2,1,0:T(8,128)S(1)} %get-tuple-element.19), kind=kOutput, calls=%fused_computation.44 | convolution fusion | flops 179758224 | bytes 13012992 | tf_op jit(solution)/shard_map/whst,wthe->wshe/dot_general | solution.py:86
  175.3 17.1 %fusion.41 = bf16[8,8,64,144]{3,2,1,0:T(8,128)(2,1)} fusion(bf16[8,144,8,64]{1,3,2,0:T(8,128)(2,1)} %bitcast.123, f32[8,8,144,144]{2,3,1,0:T(8,128)} %fusion.68, f32[8,8,144,144]{2,3,1,0:T(8,128)} %get-tuple-element.20, f32[8,8,144]{2,1,0:T(8,128)S(1)} %get-tuple-element.19), kind=kOutput, calls=%fused_computation.45 | convolution fusion | flops 179758224 | bytes 13012992 | tf_op jit(solution)/shard_map/whst,wshe->wthe/dot_general | solution.py:89
  192.3 7.4 %fusion.32 = bf16[8,8,64,144]{3,2,1,0:T(8,128)(2,1)} fusion(bf16[8,144,8,64]{1,3,2,0:T(8,128)(2,1)} %bitcast.115, f32[8,8,144,144]{2,3,1,0:T(8,128)} %get-tuple-element.20, f32[8,8,144]{2,1,0:T(8,128)S(1)} %get-tuple-element.19), kind=kOutput, calls=%fused_computation.42 | convolution fusion | flops 173113344 | bytes 7704576 | tf_op jit(solution)/shard_map/whst,wshe->wthe/dot_general | solution.py:81
  199.8 3.8 %copy.133 = bf16[1,8,144,512]{3,2,0,1:T(8,128)(2,1)} copy(bf16[1,8,144,512]{2,3,1,0:T(8,128)(2,1)} %bitcast.124) | data formatting | bytes 2359296 | tf_op jit(solution)/shard_map/stack | solution.py:92
  210.9 6.9 %bitcast_reduce_fusion = (f32[8,144]{1,0:T(8,128)S(1)}, f32[8,144]{1,0:T(8,128)S(1)}, f32[8,144,1024,1]{2,1,3,0:T(8,128)S(1)}) fusion(f32[8,144]{1,0:T(8,128)S(1)} %reshape.141, f32[8,144,1024]{2,1,0:T(8,128)} %reshape.132, f32[8,144]{1,0:T(8,128)S(1)} %reshape.142, bf16[3,1024,512]{2,1,0:T(8,128)(2,1)S(1)} %copy-done, bf16[1,8,144,512]{3,2,0,1:T(8,128)(2,1)} %copy.135, ...), kind=kOutput, calls=%fused_computation.11 | convolution fusion | flops 3633313792 | bytes 16140288 | tf_op jit(solution)/shard_map/jwse,jde->wsd/dot_general | solution.py:96
  217.9 4.1 %fusion.8 = bf16[8,144,1024]{2,1,0:T(8,128)(2,1)} fusion(f32[8,144,1024,1]{2,1,3,0:T(8,128)S(1)} %get-tuple-element.21, f32[8,144,1024]{2,1,0:T(8,128)} %reshape.132, f32[8,144]{1,0:T(8,128)S(1)} %get-tuple-element.22, f32[8,144]{1,0:T(8,128)S(1)} %get-tuple-element.23, f32[8,144]{1,0:T(8,128)S(1)} %reshape.142, f32[8,144]{1,0:T(8,128)S(1)} %reshape.141), kind=kLoop, calls=%fused_computation.14 | loop fusion | flops 8257536 | bytes 11814912 | tf_op jit(solution)/shard_map/convert_element_type | solution.py:291
  221.9 5.9 %convert_element_type.110 = bf16[4,2,6,12,2,1024]{5,4,3,2,1,0:T(2,128)(2,1)} reshape(bf16[8,144,1024]{2,1,0:T(8,128)(2,1)} %fusion.8) | data formatting | bytes 4718592 | tf_op jit(solution)/shard_map/convert_element_type | solution.py:291
  227.9 3.9 %copy.136 = bf16[4,2,6,12,2,1024]{5,4,3,1,2,0:T(2,128)(2,1)S(1)} copy(bf16[4,2,6,12,2,1024]{5,4,3,2,1,0:T(2,128)(2,1)} %convert_element_type.110) | data formatting | bytes 4718592 | tf_op jit(solution)/shard_map/convert_element_type | solution.py:291
  233.9 5.3 %fusion.35 = bf16[8,8,64,144]{3,2,1,0:T(8,128)(2,1)S(1)} fusion(bf16[8,144,8,64]{1,3,2,0:T(8,128)(2,1)} %bitcast.113, f32[8,8,144,144]{2,3,1,0:T(8,128)} %get-tuple-element.20, f32[8,8,144]{2,1,0:T(8,128)S(1)} %get-tuple-element.19), kind=kOutput, calls=%fused_computation.43 | convolution fusion | flops 173113344 | bytes 7704576 | tf_op jit(solution)/shard_map/whst,wthe->wshe/dot_general | solution.py:71
  241.9 8.5 %fusion.20 = bf16[3,1024,512]{1,2,0:T(8,128)(2,1)} fusion(bf16[1,8,144,512]{3,2,0,1:T(8,128)(2,1)S(1)} %copy-done.8, bf16[1,8,144,512]{3,2,0,1:T(8,128)(2,1)S(1)} %copy-done.7, bf16[1,8,144,512]{3,2,0,1:T(8,128)(2,1)S(1)} %copy-done.6, f32[8,144,1024]{2,1,0:T(8,128)} %reshape.132, f32[8,144]{1,0:T(8,128)S(1)} %reshape.142, f32[8,144]{1,0:T(8,128)S(1)} %reshape.141), kind=kOutput, calls=%fused_computation.28 | convolution fusion | flops 3632529408 | bytes 11412480 | tf_op jit(solution)/shard_map/wsd,jwse->jde/dot_general | solution.py:93
  253.0 4.5 %fusion.66 = (bf16[2,1024,512]{1,2,0:T(8,128)(2,1)}, bf16[2,1024,512]{1,2,0:T(8,128)(2,1)}) fusion(bf16[3,1024,512]{1,2,0:T(8,128)(2,1)} %fusion.20, bf16[1,1024,512]{1,2,0:T(8,128)(2,1)} %fusion.44), kind=kLoop, calls=%fused_computation.87 | loop fusion | flops 1048576 | bytes 10485760 | tf_op jit(solution)/shard_map/slice | solution.py:305
  257.5 4.2 %copy.146 = bf16[2,1024,512]{2,1,0:T(8,128)(2,1)} copy(bf16[2,1024,512]{1,2,0:T(8,128)(2,1)} %get-tuple-element.18) | data formatting | bytes 4194304 | tf_op jit(solution)/shard_map/slice | solution.py:305
  264.8 4.0 %copy.141 = bf16[2,1024,512]{2,1,0:T(8,128)(2,1)} copy(bf16[2,1024,512]{1,2,0:T(8,128)(2,1)} %get-tuple-element.17) | data formatting | bytes 4194304 | tf_op jit(solution)/shard_map/slice | solution.py:305
  271.4 44.1 %reduce_weights.1 = f32[4,32,512]{2,1,0:T(8,128)S(1)} custom-call(bf16[2,2,4,4,64,512]{5,4,3,2,1,0:T(8,128)(2,1)S(1)} %pad_maximum_fusion.grads), custom_call_target="tpu_custom_call" | custom-call | tf_op jit(solution)/shard_map/reduce_weights/pallas_call | solution.py:222
  318.2 4.4 %collective-permute-done.7 = bf16[3,24,1,1024]{3,1,0,2:T(8,128)(2,1)S(1)} collective-permute-done((bf16[3,24,1,1024]{3,1,0,2:T(8,128)(2,1)S(1)}, bf16[3,24,1,1024]{3,1,0,2:T(8,128)(2,1)S(1)}, u32[]{:S(2)}, u32[]{:S(2)}) %collective-permute-start.7) | collective-permute-done | bytes 147488 | tf_op jit(solution)/shard_map/ppermute | solution.py:19
  (92 shorter events, 71.1 us)
Async XLA Ops:
  7.2 93.1 %copy-start = (bf16[3,1024,512]{2,1,0:T(8,128)(2,1)S(1)}, bf16[3,1024,512]{2,1,0:T(8,128)(2,1)}, u32[]{:S(2)}) copy-start(bf16[3,1024,512]{2,1,0:T(8,128)(2,1)} %param.7) | copy-start | bytes 9437188
  7.2 64.2 %all-gather.3.cloned.1.call-start = ((), (), s32[]{:S(2)}) async-start(), calls=%async_computation.1 | async-start | bytes 3538944 | tf_op jit(solution)/shard_map/all_gather | solution.py:271
  8.3 5.9 %collective-permute-start = (bf16[3,24,1,1024]{3,1,2,0:T(8,128)(2,1)S(1)}, bf16[3,24,1,1024]{3,1,2,0:T(8,128)(2,1)S(1)}, u32[]{:S(2)}, u32[]{:S(2)}) collective-permute-start(bf16[3,24,1,1024]{3,1,2,0:T(8,128)(2,1)S(1)} %slice.82), channel_id=1, source_target_pairs={{64,0},{0,64},{65,1},{1,65},{66,2},{2,66},{67,3},{3,67},{68,4},{4,... | collective-permute-start | bytes 442376 | tf_op jit(solution)/shard_map/ppermute | solution.py:19
  14.3 15.9 %collective-permute-start.1 = (bf16[24,6,1,1024]{3,1,2,0:T(8,128)(2,1)S(1)}, bf16[24,6,1,1024]{3,1,2,0:T(8,128)(2,1)S(1)}, u32[]{:S(2)}, u32[]{:S(2)}) collective-permute-start(bf16[24,6,1,1024]{3,1,2,0:T(8,128)(2,1)S(1)} %pad_maximum_fusion.9), channel_id=1, source_target_pairs={{2,0},{4,2},{6,4},{8,6},{10,8},{12,10},{14,12},{16,14},{18,16},{20... | collective-permute-start | bytes 884744 | tf_op jit(solution)/shard_map/ppermute | solution.py:19
  23.0 8.5 %copy-start.10 = (s32[24,24,1]{1,2,0:T(1,128)S(1)}, s32[24,24,1]{1,2,0:T(1,128)}, u32[]{:S(2)}) copy-start(s32[24,24,1]{1,2,0:T(1,128)} %param.6) | copy-start | bytes 6916
  31.5 87.9 %all-gather.5.cloned.1.call-start = ((), (), s32[]{:S(2)}) async-start(), calls=%async_computation.2 | async-start | bytes 3538944 | tf_op jit(solution)/shard_map/all_gather | solution.py:273
  32.1 6.9 %collective-permute-start.2 = (s32[3,24,1]{1,0,2:T(4,128)}, s32[3,24,1]{1,0,2:T(4,128)S(1)}, u32[]{:S(2)}, u32[]{:S(2)}) collective-permute-start(s32[3,24,1]{1,0,2:T(4,128)} %slice.109), channel_id=1, source_target_pairs={{64,0},{0,64},{65,1},{1,65},{66,2},{2,66},{67,3},{3,67},{68,4},{4,... | collective-permute-start | bytes 872 | tf_op jit(solution)/shard_map/ppermute | solution.py:19
  34.7 17.2 %collective-permute-start.4 = (bf16[3,24,1,1024]{3,1,2,0:T(8,128)(2,1)}, bf16[3,24,1,1024]{3,1,2,0:T(8,128)(2,1)}, u32[]{:S(2)}, u32[]{:S(2)}) collective-permute-start(bf16[3,24,1,1024]{3,1,2,0:T(8,128)(2,1)} %slice.92), channel_id=1, source_target_pairs={{64,0},{0,64},{65,1},{1,65},{66,2},{2,66},{67,3},{3,67},{68,4},{4,... | collective-permute-start | bytes 442376 | tf_op jit(solution)/shard_map/ppermute | solution.py:19
  39.7 9.6 %collective-permute-start.3 = (s32[24,6,1]{1,0,2:T(8,128)S(1)}, s32[24,6,1]{1,0,2:T(8,128)S(1)}, u32[]{:S(2)}, u32[]{:S(2)}) collective-permute-start(s32[24,6,1]{1,0,2:T(8,128)S(1)} %pad_add_fusion), channel_id=1, source_target_pairs={{2,0},{4,2},{6,4},{8,6},{10,8},{12,10},{14,12},{16,14},{18,16},{20... | collective-permute-start | bytes 1736 | tf_op jit(solution)/shard_map/ppermute | solution.py:19
  51.9 10.3 %copy-start.2 = (bf16[21,24,1,1024]{3,1,2,0:T(8,128)(2,1)S(1)}, bf16[21,24,1,1024]{3,1,2,0:T(8,128)(2,1)}, u32[]{:S(2)}) copy-start(bf16[21,24,1,1024]{3,1,2,0:T(8,128)(2,1)} %slice.91) | copy-start | bytes 3096580
  53.1 16.8 %collective-permute-start.5 = (bf16[24,6,1,1024]{3,1,2,0:T(8,128)(2,1)S(1)}, bf16[24,6,1,1024]{3,1,2,0:T(8,128)(2,1)S(1)}, u32[]{:S(2)}, u32[]{:S(2)}) collective-permute-start(bf16[24,6,1,1024]{3,1,2,0:T(8,128)(2,1)S(1)} %pad_maximum_fusion.8), channel_id=1, source_target_pairs={{2,0},{4,2},{6,4},{8,6},{10,8},{12,10},{14,12},{16,14},{18,16},{20... | collective-permute-start | bytes 884744 | tf_op jit(solution)/shard_map/ppermute | solution.py:19
  71.2 179.2 %reduce-scatter.2.cloned.1.call-start = ((), (), s32[]{:S(2)}) async-start(), calls=%async_computation.3 | async-start | bytes 3538944 | tf_op jit(solution)/shard_map/reduce_scatter | solution.py:290
  75.5 2.2 copy-start.1
  141.4 7.4 %copy-start.9 = (pred[8,144,144]{1,2,0:T(8,128)(4,1)S(1)}, pred[8,144,144]{1,2,0:T(8,128)(4,1)}, u32[]{:S(2)}) copy-start(pred[8,144,144]{1,2,0:T(8,128)(4,1)} %or_and_fusion) | copy-start | bytes 497668
  233.9 5.3 %copy-start.5 = (bf16[8,144,1024]{2,1,0:T(8,128)(2,1)S(1)}, bf16[8,144,1024]{2,1,0:T(8,128)(2,1)}, u32[]{:S(2)}) copy-start(bf16[8,144,1024]{2,1,0:T(8,128)(2,1)} %reshape.129) | copy-start | bytes 7077892
  239.3 2.6 copy-start.6
  239.3 2.6 copy-start.7
  239.3 2.6 copy-start.8
  251.6 64.5 %collective-permute-start.6 = (bf16[24,6,1,1024]{3,0,2,1:T(8,128)(2,1)S(1)}, bf16[24,6,1,1024]{3,0,2,1:T(8,128)(2,1)}, u32[]{:S(2)}, u32[]{:S(2)}) collective-permute-start(bf16[24,6,1,1024]{3,0,2,1:T(8,128)(2,1)S(1)} %copy.138), channel_id=1, source_target_pairs={{62,0},{0,2},{2,4},{4,6},{6,8},{8,10},{10,12},{12,14},{14,16},{16,... | collective-permute-start | bytes 884744 | tf_op jit(solution)/shard_map/ppermute | solution.py:19
  271.4 45.9 %copy-start.3 = (bf16[24,24,1,1024]{3,1,0,2:T(8,128)(2,1)S(1)}, bf16[24,24,1,1024]{3,1,0,2:T(8,128)(2,1)}, u32[]{:S(2)}) copy-start(bf16[24,24,1,1024]{3,1,0,2:T(8,128)(2,1)} %reduce-scatter.2.cloned.1.call-done) | copy-start | bytes 3538948
  315.4 7.1 %copy-start.4 = (bf16[24,24,1,1024]{3,1,2,0:T(8,128)(2,1)S(1)}, bf16[24,24,1,1024]{3,1,2,0:T(8,128)(2,1)}, u32[]{:S(2)}) copy-start(bf16[24,24,1,1024]{3,1,2,0:T(8,128)(2,1)} %param.9) | copy-start | bytes 3538948
  317.4 5.2 %collective-permute-start.7 = (bf16[3,24,1,1024]{3,1,0,2:T(8,128)(2,1)S(1)}, bf16[3,24,1,1024]{3,1,0,2:T(8,128)(2,1)S(1)}, u32[]{:S(2)}, u32[]{:S(2)}) collective-permute-start(bf16[3,24,1,1024]{3,1,0,2:T(8,128)(2,1)S(1)} %pad_maximum_fusion.10), channel_id=1, source_target_pairs={{64,0},{0,64},{65,1},{1,65},{66,2},{2,66},{67,3},{3,67},{68,4},{4,... | collective-permute-start | bytes 442376 | tf_op jit(solution)/shard_map/ppermute | solution.py:19
Sparse Core Ops, SparseCore 0:
  31.6 15.2 all-gather.2
  71.3 15.2 all-gather.4
  234.0 14.2 reduce-scatter.1

commit v2 on v0

v2 whole, which is shorter than its diff:
```python
import jax
import jax.numpy as jnp
import numpy as np
from jax import lax
from jax.experimental import pallas as pl
from jax.experimental.pallas import tpu as pltpu
from jax.sharding import PartitionSpec as P

f32, bf16 = jnp.float32, jnp.bfloat16
MESH = pl.DeviceIdType.MESH
NN = (((1,), (0,)), ((), ()))
NT = (((1,), (1,)), ((), ()))

D = 1024
HEADS = 4
GROUP = HEADS * 64
PASSES = 2
ROWS = COLS = 24
OWN = ROWS * COLS
WINDOWS = 8
LEVEL = 72
SEQ = 2 * LEVEL
SLOT = 80
LOCAL = 3
WIDE = D + 128
A_ROWS, C_ROWS, B_ROWS = 128, 32, 64
HALO = A_ROWS + C_ROWS + B_ROWS
PARTS = ((0, A_ROWS), (A_ROWS, C_ROWS), (A_ROWS + C_ROWS, B_ROWS))
BAND_START = (64, 208, 352, 416)


def selections():
    send = np.zeros((HALO, OWN), np.float32)
    for r in range(ROWS):
        for c in range(COLS):
            if r >= 3 and c < 6:
                send[(r - 3) * 6 + c, r * COLS + c] = 1
            elif r < 3 and c < 6:
                send[A_ROWS + r * 6 + c, r * COLS + c] = 1
            elif r < 3:
                send[A_ROWS + C_ROWS + r * 18 + c - 6, r * COLS + c] = 1
    own = np.zeros((WINDOWS, SLOT, 160), np.float32)
    halo = np.zeros((WINDOWS, SLOT, HALO), np.float32)
    for j in range(2):
        for b in range(4):
            w = j * 4 + b
            for i in range(6):
                for c in range(12):
                    t, r, col = i * 12 + c, 6 * b + i, 12 * j + c
                    if r < 21 and col < 18:
                        own[w, t, (r + 3) * COLS + col + 6 - BAND_START[b]] = 1
                    elif r < 21:
                        halo[w, t, r * 6 + col - 18] = 1
                    elif col >= 18:
                        halo[w, t, A_ROWS + (r - 21) * 6 + col - 18] = 1
                    else:
                        halo[w, t, A_ROWS + C_ROWS + (r - 21) * 18 + col] = 1
    own = own[[0, 3, 4, 7]]
    halo = halo[3:]
    swap = lambda a: np.ascontiguousarray(np.swapaxes(a, -1, -2))
    return [a.astype(jnp.bfloat16) for a in (send, swap(send), own, swap(own), halo, swap(halo))]


def own_kind(w):
    return (0, 0, 0, 1, 2, 2, 2, 3)[w]


def dot(a, b, dims=NN):
    return lax.dot_general(a, b, dims, preferred_element_type=f32)


def place():
    lat, lon, tp = (lax.axis_index(a) for a in ("lat", "lon", "tp"))
    return lon // 8, (lon // 2) % 4, (lon % 2) * 2 + lat, tp


def device_at(y, x, z, tp):
    return (z % 2, (y * 4 + x) * 2 + z // 2, tp)


def kernel(
    x, g, mask, wq, wo, send_m, send_t, own_m, own_t, halo_m, halo_t,
    dtok, dw,
    nat, mean, rstd, out_n, out_g, in_n, in_g, nw, gw, nf, gf, n_t, g_t, bias, qkv, da, att, dp,
    grads, got1, mid1, got2, mid2, got3,
    mine, back_out, back_in, total, ret_out, ret_in, local,
    halo_s, halo_r, core_s, core_r, ret_s, ret_r, back_s, back_r, red_s, red_r,
):
    y, px, z, tp = place()
    lat, lon = lax.axis_index("lat"), lax.axis_index("lon")
    other = (lat, lon, 1 - tp)
    before, after = (lon + 31) % 32, (lon + 1) % 32
    along_y = [device_at((y + d) % 4, px, z, tp) for d in (1, 2, 3)]
    along_x = [device_at(y, (px + d) % 4, z, tp) for d in (1, 2, 3)]
    along_z = [device_at(y, px, (z + d) % 4, tp) for d in (1, 2, 3)]
    to_a, to_c, to_b = (lat, before, tp), (1 - lat, before, tp), (1 - lat, lon, tp)
    from_a, from_c = (lat, after, tp), (1 - lat, after, tp)

    barrier = pltpu.get_barrier_semaphore()
    greeted = [other, to_a, to_c, from_a, from_c] + along_y + along_x + along_z
    for peer in greeted:
        pl.semaphore_signal(barrier, inc=1, device_id=peer, device_id_type=MESH)

    def copy(src, dst, s, r, peer):
        return pltpu.make_async_remote_copy(
            src_ref=src, dst_ref=dst, send_sem=s, recv_sem=r, device_id=peer, device_id_type=MESH
        )

    @pl.loop(0, OWN // 64)
    def _(i):
        rows = pl.ds(pl.multiple_of(i * 64, 64), 64)
        v = x[rows, :].astype(f32)
        m = jnp.mean(v, axis=-1, keepdims=True)
        v = v - m
        s = lax.rsqrt(jnp.mean(v * v, axis=-1, keepdims=True) + 1e-05)
        mean[rows, :] = m
        rstd[rows, :] = s
        nat[rows, :D] = (v * s).astype(bf16)
        nat[rows, D:] = mask[rows, :]

    out_n[...] = dot(send_m[...], nat[...]).astype(bf16)
    out_g[...] = dot(send_m[...], g[...]).astype(bf16)
    pl.semaphore_wait(barrier, len(greeted))

    halos = []
    for i, ((start, size), peer) in enumerate(zip(PARTS, (to_a, to_c, to_b))):
        rows = pl.ds(start, size)
        halos.append(copy(out_n.at[rows], in_n.at[rows], halo_s.at[0, i], halo_r.at[0, i], peer))
        halos.append(copy(out_g.at[rows], in_g.at[rows], halo_s.at[1, i], halo_r.at[1, i], peer))
    for c in halos:
        c.start()

    def exchanges(w):
        return (
            copy(nw.at[tp, w], nw.at[tp, w], core_s.at[0, w], core_r.at[0, w], other),
            copy(gw.at[tp, w], gw.at[tp, w], core_s.at[1, w], core_r.at[1, w], other),
        )

    def assemble(w):
        rows = pl.ds(BAND_START[w % 4], 160)
        n, c = dot(own_m[own_kind(w)], nat[rows, :]), dot(own_m[own_kind(w)], g[rows, :])
        if w >= LOCAL:
            n += dot(halo_m[w - LOCAL], in_n[...])
            c += dot(halo_m[w - LOCAL], in_g[...])
        nw[tp, w] = n.astype(bf16)
        gw[tp, w] = c.astype(bf16)
        for e in exchanges(w):
            e.start()

    def gather(w):
        for e in exchanges(w):
            e.wait_recv()
        rows = pl.ds(pl.multiple_of(w * SEQ, 16), SEQ)
        n = jnp.concatenate([nw[i, w].astype(f32)[:LEVEL] for i in (0, 1)])
        nf[rows, :] = n[:, :D].astype(bf16)
        gf[rows, :] = jnp.concatenate([gw[i, w].astype(f32)[:LEVEL] for i in (0, 1)]).astype(bf16)
        keys = jnp.concatenate([n[:, D:], n[:, D : D + SEQ - 128]], axis=1)
        t = lax.broadcasted_iota(jnp.int32, (SEQ, SEQ), 0)
        s = lax.broadcasted_iota(jnp.int32, (SEQ, SEQ), 1)
        region = lambda i: jnp.where(i >= LEVEL, i - LEVEL, i) >= LEVEL // 2
        last = ((w % 4) == 3).astype(jnp.int32) * lat
        crossing = jnp.where(region(t) != region(s), 1, 0) * last
        open_key = jnp.where(t == s, 1.0, keys)
        bias[w] = jnp.where((open_key == 1.0) & (crossing == 0), 0.0, -1e30)

    def project(p, start, size):
        rows, c = pl.ds(start, size), pl.ds(p * GROUP, GROUP)
        n = nf[rows, :]
        for j in range(3):
            o = dot(n, wq[j, :, c]).astype(bf16)
            qkv[j, rows, :] = o * bf16(0.125) if j == 0 else o
        da[rows, :] = dot(gf[rows, :], wo[c, :], NT).astype(bf16)

    lane = lax.broadcasted_iota(jnp.int32, (1, GROUP), 1) // 64
    heads = [(lane == h).astype(f32).astype(bf16) for h in range(HEADS)]

    def attend(p, w):
        rows, c = pl.ds(pl.multiple_of(w * SEQ, 16), SEQ), pl.ds(p * GROUP, GROUP)
        q, k, v, d = qkv[0, rows, :], qkv[1, rows, :], qkv[2, rows, :], da[rows, :]
        b = bias[w]
        v_t, k_t = v.T, k.T
        scores = dot(jnp.concatenate([k * m for m in heads]), q, NT)
        d_probs = dot(jnp.concatenate([v * m for m in heads]), d, NT)
        d_v, d_k = jnp.zeros((SEQ, GROUP), f32), jnp.zeros((SEQ, GROUP), f32)
        out_t, d_q_t = [], []
        for h in range(HEADS):
            s = scores[SEQ * h : SEQ * h + SEQ] + b
            e = jnp.exp(s - jnp.max(s, axis=0, keepdims=True))
            pr = e * (1.0 / jnp.sum(e, axis=0, keepdims=True))
            pb = pr.astype(bf16)
            u = pr * d_probs[SEQ * h : SEQ * h + SEQ]
            ds = (u - pr * jnp.sum(u, axis=0, keepdims=True)).astype(bf16)
            out_t.append(dot(v_t[64 * h : 64 * h + 64], pb))
            d_q_t.append(dot(k_t[64 * h : 64 * h + 64], ds))
            d_v += dot(pb, d * heads[h])
            d_k += dot(ds, q * heads[h])
        att[rows, c] = jnp.concatenate(out_t).astype(bf16).T
        dp[0, rows, c] = (jnp.concatenate(d_q_t) * 0.125).astype(bf16).T
        dp[1, rows, c] = d_k.astype(bf16)
        dp[2, rows, c] = d_v.astype(bf16)

    first, second = (y, px), (px, y)
    peers = ((along_y, along_x), (along_x, along_y))

    def stage(n, p, color, d):
        sems = (red_s.at[p, color, n, d - 1], red_r.at[p, color, n, d - 1])
        if n == 0:
            src = grads.at[p, color, (first[color] + d) % 4]
            return copy(src, got1.at[p, color, d - 1], *sems, peers[color][0][d - 1])
        if n == 1:
            src = mid1.at[p, color, (second[color] + d) % 4]
            return copy(src, got2.at[p, color, d - 1], *sems, peers[color][1][d - 1])
        src = mid2.at[p, color, ((z + d) % 4) // 2]
        return copy(src, got3.at[p, z, color], *sems, along_z[d - 1])

    def weight_grads(p):
        c = pl.ds(p * GROUP, GROUP)
        for d in (1, 2, 3, 0):
            row = (y + d) % 4
            a = n_t[pl.ds(pl.multiple_of(row * 256, 256), 256), :]
            col = (px + d) % 4
            pieces = [pl.ds(pl.multiple_of(i * 256 + col * 64, 64), 64) for i in range(4)]
            b = jnp.concatenate([n_t[i, :] for i in pieces])
            e = jnp.concatenate([g_t[i, :] for i in pieces])
            for color, m, val in (
                (0, 0, dot(a, dp[0, :, c])),
                (0, 1, dot(a, dp[1, :, c])),
                (1, 0, dot(b, dp[2, :, c])),
                (1, 1, dot(e, att[:, c])),
            ):
                val = val.astype(bf16)
                for i in range(4):
                    grads[p, color, (row, col)[color], i, m] = val[64 * i : 64 * i + 64]
            if d:
                stage(0, p, 0, d).start()
                stage(0, p, 1, d).start()

    def reduce_first(p):
        for color in (0, 1):
            for d in (1, 2, 3):
                stage(0, p, color, d).wait_recv()

            @pl.loop(0, 4)
            def _(i):
                s = grads[p, color, first[color], i].astype(f32)
                for d in range(3):
                    s += got1[p, color, d, i].astype(f32)
                mid1[p, color, i] = s.astype(bf16)

            for d in (1, 2, 3):
                stage(1, p, color, d).start()

    def reduce_second(p):
        for color in (0, 1):
            for d in (1, 2, 3):
                stage(1, p, color, d).wait_recv()
            s = mid1[p, color, second[color]].astype(f32)
            for d in range(3):
                s += got2[p, color, d].astype(f32)
            s = s.astype(bf16)
            mid2[p, color, 0] = s[:, :32]
            mid2[p, color, 1] = s[:, 32:]
            got3[p, z, color] = mid2[p, color, z // 2]
            for d in (1, 2, 3):
                stage(2, p, color, d).start()

    def reduce_third(p):
        for color in (0, 1):
            for d in (1, 2, 3):
                stage(2, p, color, d).wait_recv()
            s = got3[p, 0, color].astype(f32)
            for i in range(1, 4):
                s += got3[p, i, color].astype(f32)
            for m in range(2):
                dw[2 * color + m, :, p * GROUP : p * GROUP + GROUP] = s[m]

    for w in range(LOCAL):
        assemble(w)
    pl.loop(0, LOCAL)(gather)
    for p in range(PASSES):
        project(p, 0, LOCAL * SEQ)
        pl.loop(0, LOCAL)(lambda w, p=p: attend(p, w))
    for c in halos:
        c.wait_recv()
    for w in range(LOCAL, WINDOWS):
        assemble(w)
    pl.loop(LOCAL, WINDOWS)(gather)
    for i in range(9):
        rows = pl.ds(i * 128, 128)
        n_t[:, i * 128 : i * 128 + 128] = nf[rows, :].T
        g_t[:, i * 128 : i * 128 + 128] = gf[rows, :].T
    for p in range(PASSES):
        project(p, LOCAL * SEQ, (WINDOWS - LOCAL) * SEQ)
        pl.loop(LOCAL, WINDOWS)(lambda w, p=p: attend(p, w))
        if p:
            reduce_first(p - 1)
        weight_grads(p)
        if p:
            reduce_second(p - 1)

    def returned(w):
        return copy(back_out.at[w], back_in.at[w], back_s.at[w], back_r.at[w], other)

    def d_normed(w):
        rows = pl.ds(pl.multiple_of(w * SEQ, 16), SEQ)
        o = sum(dot(dp[j, rows, :], wq[j], NT) for j in range(3))
        pad = jnp.zeros((SLOT - LEVEL, D), f32)
        lo, hi = jnp.concatenate([o[:LEVEL], pad]), jnp.concatenate([o[LEVEL:], pad])
        mine[w] = jnp.where(tp == 0, lo, hi)
        back_out[w] = jnp.where(tp == 0, hi, lo).astype(bf16)
        returned(w).start()

    pl.loop(LOCAL, WINDOWS)(d_normed)
    pl.loop(0, LOCAL)(d_normed)
    reduce_first(PASSES - 1)

    def add(w):
        returned(w).wait_recv()
        total[w] = (mine[w] + back_in[w].astype(f32)).astype(bf16)

    pl.loop(LOCAL, WINDOWS)(add)
    ret_out[...] = sum(dot(halo_t[w - LOCAL], total[w]) for w in range(LOCAL, WINDOWS)).astype(bf16)
    returns = []
    for i, ((start, size), peer) in enumerate(zip(PARTS, (from_a, from_c, to_b))):
        rows = pl.ds(start, size)
        returns.append(copy(ret_out.at[rows], ret_in.at[rows], ret_s.at[i], ret_r.at[i], peer))
    for c in returns:
        c.start()
    pl.loop(0, LOCAL)(add)
    local[:LEVEL] = jnp.zeros((LEVEL, D), f32)
    for b in range(4):
        o = dot(own_t[own_kind(b)], total[b]) + dot(own_t[own_kind(b + 4)], total[b + 4])
        skip = 72 + 144 * b - BAND_START[b]
        size = 144 if b < 3 else 72
        local[72 + 144 * b : 72 + 144 * b + size] = o[skip : skip + size]
    reduce_second(PASSES - 1)
    for c in returns:
        c.wait_recv()

    @pl.loop(0, 4)
    def _(i):
        rows = pl.ds(pl.multiple_of(i * 144, 16), 144)
        dn = local[rows, :] + dot(send_t[rows, :], ret_in[...])
        s = rstd[rows, :]
        xh = (x[rows, :].astype(f32) - mean[rows, :]) * s
        inner = dn - jnp.mean(dn, axis=-1, keepdims=True) - xh * jnp.mean(dn * xh, axis=-1, keepdims=True)
        dtok[rows, :] = (s * inner + g[rows, :].astype(f32)).astype(bf16)

    for p in range(PASSES):
        reduce_third(p)
    for c in halos + returns:
        c.wait_send()

    @pl.loop(0, WINDOWS)
    def _(w):
        for e in exchanges(w):
            e.wait_send()
        returned(w).wait_send()

    for p in range(PASSES):
        for n in range(3):
            for color in (0, 1):
                for d in (1, 2, 3):
                    stage(n, p, color, d).wait_send()


def body(tokens, land_mask, qkv_weight, out_weight, out_grad):
    mask = jnp.broadcast_to(land_mask.reshape(OWN, 1).astype(bf16), (OWN, 128))
    constants = [jnp.asarray(a) for a in selections()]
    operands = [tokens.reshape(OWN, D), out_grad.reshape(OWN, D), mask, qkv_weight, out_weight] + constants
    vmem, dma = pltpu.VMEM, pltpu.SemaphoreType.DMA
    tokens_all = WINDOWS * SEQ
    d_tokens, d_weights = pl.pallas_call(
        kernel,
        out_shape=(jax.ShapeDtypeStruct((OWN, D), bf16), jax.ShapeDtypeStruct((4, 32, 512), f32)),
        in_specs=[pl.BlockSpec(memory_space=pltpu.VMEM)] * len(operands),
        out_specs=[pl.BlockSpec(memory_space=pltpu.VMEM)] * 2,
        scratch_shapes=[
            vmem((OWN, WIDE), bf16),
            vmem((OWN, 1), f32),
            vmem((OWN, 1), f32),
            vmem((HALO, WIDE), bf16),
            vmem((HALO, D), bf16),
            vmem((HALO, WIDE), bf16),
            vmem((HALO, D), bf16),
            vmem((2, WINDOWS, SLOT, WIDE), bf16),
            vmem((2, WINDOWS, SLOT, D), bf16),
            vmem((tokens_all, D), bf16),
            vmem((tokens_all, D), bf16),
            vmem((D, tokens_all), bf16),
            vmem((D, tokens_all), bf16),
            vmem((WINDOWS, SEQ, SEQ), f32),
            vmem((3, tokens_all, GROUP), bf16),
            vmem((tokens_all, GROUP), bf16),
            vmem((tokens_all, 512), bf16),
            vmem((3, tokens_all, 512), bf16),
            vmem((PASSES, 2, 4, 4, 2, 64, GROUP), bf16),
            vmem((PASSES, 2, 3, 4, 2, 64, GROUP), bf16),
            vmem((PASSES, 2, 4, 2, 64, GROUP), bf16),
            vmem((PASSES, 2, 3, 2, 64, GROUP), bf16),
            vmem((PASSES, 2, 2, 2, 32, GROUP), bf16),
            vmem((PASSES, 4, 2, 2, 32, GROUP), bf16),
            vmem((WINDOWS, SLOT, D), f32),
            vmem((WINDOWS, SLOT, D), bf16),
            vmem((WINDOWS, SLOT, D), bf16),
            vmem((WINDOWS, SLOT, D), bf16),
            vmem((HALO, D), bf16),
            vmem((HALO, D), bf16),
            vmem((OWN, D), f32),
            dma((2, 3)),
            dma((2, 3)),
            dma((2, WINDOWS)),
            dma((2, WINDOWS)),
            dma((3,)),
            dma((3,)),
            dma((WINDOWS,)),
            dma((WINDOWS,)),
            dma((PASSES, 2, 3, 3)),
            dma((PASSES, 2, 3, 3)),
        ],
        compiler_params=pltpu.CompilerParams(
            collective_id=0, has_side_effects=True, vmem_limit_bytes=63 * 1024 * 1024
        ),
        name="swin_backward",
    )(*operands)
    return d_tokens.reshape(ROWS, COLS, 1, D), d_weights[:3], d_weights[3].T


def solution(mesh):
    in_specs = (
        P("lat", "lon", "tp", None),
        P("lat", "lon", "tp"),
        P(None, None, "tp"),
        P("tp", None),
        P("lat", "lon", "tp", None),
    )
    out_specs = (P("lat", "lon", "tp", None), P(None, "lon", "tp"), P("tp", "lon"))
    return jax.shard_map(body, mesh=mesh, in_specs=in_specs, out_specs=out_specs, check_vma=False)
```

time: 856 us -> 100 us (0.12)
  waiting for transfers between devices: 577 us -> 0 us
  matrix products: 94.1 us -> 0 us
  Pallas kernels: 0 us -> 91.7 us
  local copies, waits for them, and re-layouts: 95.3 us -> 6.36 us
  starting transfers between devices: 30.2 us -> 0 us
  other arithmetic: 27.5 us -> 0.75 us
  between operations: 15.3 us -> 0.64 us
  blocking collectives: 10.6 us -> 0 us
    unnamed x7 -> x0, waiting for transfers between devices: 342 us -> none
    reduce_scatter x2 -> x0, waiting for transfers between devices: 187 us -> none  [the longest x1 187 us: body(): lax.psum_scatter(d_out.astype(jnp.bfloat16), 'lon', scatter_dimension=1,...]
    pallas_call x0 -> x1, Pallas kernels: none -> 91.7 us  [body(): pl.pallas_call(kernel, out_shape=(jax.ShapeDtypeStruct((OWN, D), bf16), j...]
    dot_general x10 -> x0, matrix products: 84.6 us -> none  [the longest x1 16.9 us: window_grads(): jnp.einsum('whst,wthe->wshe', d_scores, key_rows, preferred_element_type=...]
    convert_element_type x7 -> x1, local copies, waits for them, and re-layouts: 35 us -> 0.1 us  [body(): mask = jnp.broadcast_to(land_mask.reshape(OWN, 1).astype(bf16), (OWN, 128))]
    ppermute x8 -> x0, waiting for transfers between devices: 32.8 us -> none  [shifted(): return lax.ppermute(block, axis, route)]
    ppermute x8 -> x0, starting transfers between devices: 29.5 us -> none  [shifted(): return lax.ppermute(block, axis, route)]
    psum x1 -> x0, waiting for transfers between devices: 15.3 us -> none  [body(): lax.psum(sector_part[0].astype(jnp.bfloat16), 'lat').astype(jnp.float32)]
  transfers between devices with their start and end apart: 14 -> 0, of which waited for: 8 -> 0; matrix products, arithmetic and copies ran while one was open for 11% -> 0% of each run, Pallas kernels for 0% -> 0%
where the time goes in v2:
time: 100 us; the launch traced here: 99.4 us
  Pallas kernels  91.7 us (92%)
  local copies, waits for them, and re-layouts  6.36 us (6%)
    pallas_call x1, Pallas kernels, body(): pl.pallas_call(kernel, out_shape=(jax.ShapeDtypeStruct((OWN, D), bf16), j...  91.7 us
    unnamed x1, local copies, waits for them, and re-layouts  2.37 us

profile of v2, /device:TPU:0, one launch (start us, length us, event | category | flops | bytes accessed | tf_op | source)
XLA Modules:
  0.0 99.4 jit_solution(15102807554120517905)
XLA Ops:
  0.6 0.8 convert_reduce_fusion
  1.4 0.1 convert_element_type.12
  1.5 0.8 broadcast_in_dim.2.mask
  2.3 91.7 %swin_backward.1 = (bf16[576,1024]{1,0:T(8,128)(2,1)}, f32[4,32,512]{2,1,0:T(8,128)}) custom-call(bf16[576,1024]{1,0:T(8,128)(2,1)} %bitcast.9, bf16[576,1024]{1,0:T(8,128)(2,1)} %bitcast.10, bf16[576,128]{1,0:T(8,128)(2,1)} %broadcast_in_dim.2.mask, bf16[3,1024,512]{2,1,0:T(8,128)(2,1)} %wq.1, bf16[512,1024]{1,0:T(8,128)(2,1)} %wo.1, ...), custom_call_target="tpu_custom_call" | custom-call | tf_op jit(solution)/shard_map/swin_backward/pallas_call | solution.py:373
  94.0 1.5 %slice_bitcast_fusion = f32[512,32]{0,1:T(8,128)} fusion(f32[4,32,512]{2,1,0:T(8,128)} %get-tuple-element.6), kind=kLoop, calls=%fused_computation | loop fusion | bytes 131072 | tf_op jit(solution)/shard_map/transpose | solution.py:426
  95.5 1.6 %slice.6 = f32[3,32,512]{2,1,0:T(8,128)} slice(f32[4,32,512]{2,1,0:T(8,128)} %get-tuple-element.6), slice={[0:3], [0:32], [0:512]} | slice | bytes 393216 | tf_op jit(solution)/shard_map/slice | solution.py:426
  97.1 2.4 %copy.16 = bf16[24,24,1,1024]{3,1,2,0:T(8,128)(2,1)} copy(bf16[24,24,1,1024]{3,1,2,0:T(8,128)(2,1)} %bitcast.11) | data formatting | bytes 2359296

commit v3 on v2

--- a/solution.py
+++ b/solution.py
@@ -21,44 +21,44 @@
 LEVEL = 72
 SEQ = 2 * LEVEL
 SLOT = 80
-LOCAL = 3
+EARLY = 4
 WIDE = D + 128
-A_ROWS, C_ROWS, B_ROWS = 128, 32, 64
-HALO = A_ROWS + C_ROWS + B_ROWS
-PARTS = ((0, A_ROWS), (A_ROWS, C_ROWS), (A_ROWS + C_ROWS, B_ROWS))
+A_ROWS, B_ROWS, C_ROWS = 128, 64, 32
+BC_ROWS = B_ROWS + C_ROWS
+HALO = A_ROWS + BC_ROWS
+PARTS = ((0, A_ROWS), (A_ROWS, B_ROWS), (A_ROWS + B_ROWS, C_ROWS))
 BAND_START = (64, 208, 352, 416)
 
 
 def selections():
     send = np.zeros((HALO, OWN), np.float32)
+    own = np.zeros((WINDOWS, SLOT, 160), np.float32)
+    cols = np.zeros((4, SLOT, A_ROWS), np.float32)
+    rest = np.zeros((2, SLOT, BC_ROWS), np.float32)
     for r in range(ROWS):
         for c in range(COLS):
             if r >= 3 and c < 6:
                 send[(r - 3) * 6 + c, r * COLS + c] = 1
-            elif r < 3 and c < 6:
-                send[A_ROWS + r * 6 + c, r * COLS + c] = 1
+            elif r < 3 and c >= 6:
+                send[A_ROWS + r * 18 + c - 6, r * COLS + c] = 1
             elif r < 3:
-                send[A_ROWS + C_ROWS + r * 18 + c - 6, r * COLS + c] = 1
-    own = np.zeros((WINDOWS, SLOT, 160), np.float32)
-    halo = np.zeros((WINDOWS, SLOT, HALO), np.float32)
+                send[A_ROWS + B_ROWS + r * 6 + c, r * COLS + c] = 1
     for j in range(2):
         for b in range(4):
-            w = j * 4 + b
             for i in range(6):
                 for c in range(12):
                     t, r, col = i * 12 + c, 6 * b + i, 12 * j + c
                     if r < 21 and col < 18:
-                        own[w, t, (r + 3) * COLS + col + 6 - BAND_START[b]] = 1
+                        own[j * 4 + b, t, (r + 3) * COLS + col + 6 - BAND_START[b]] = 1
                     elif r < 21:
-                        halo[w, t, r * 6 + col - 18] = 1
-                    elif col >= 18:
-                        halo[w, t, A_ROWS + (r - 21) * 6 + col - 18] = 1
+                        cols[b, t, r * 6 + col - 18] = 1
+                    elif col < 18:
+                        rest[j, t, (r - 21) * 18 + col] = 1
                     else:
-                        halo[w, t, A_ROWS + C_ROWS + (r - 21) * 18 + col] = 1
+                        rest[j, t, B_ROWS + (r - 21) * 6 + col - 18] = 1
     own = own[[0, 3, 4, 7]]
-    halo = halo[3:]
     swap = lambda a: np.ascontiguousarray(np.swapaxes(a, -1, -2))
-    return [a.astype(jnp.bfloat16) for a in (send, swap(send), own, swap(own), halo, swap(halo))]
+    return [a.astype(jnp.bfloat16) for a in (send, swap(send), own, swap(own), cols, swap(cols), rest, swap(rest))]
 
 
 def own_kind(w):
@@ -79,12 +79,13 @@
 
 
 def kernel(
-    x, g, mask, wq, wo, send_m, send_t, own_m, own_t, halo_m, halo_t,
-    dtok, dw,
+    x_h, g_h, mask, wq_h, wo_h, send_mh, send_th, own_mh, own_th, cols_mh, cols_th, rest_mh, rest_th,
+    dtok, dwq, dwo,
+    x, g, wq, wo, send_m, send_t, own_m, own_t, cols_m, cols_t, rest_m, rest_t,
     nat, mean, rstd, out_n, out_g, in_n, in_g, nw, gw, nf, gf, n_t, g_t, bias, qkv, da, att, dp,
-    grads, got1, mid1, got2, mid2, got3,
-    mine, back_out, back_in, total, ret_out, ret_in, local,
-    halo_s, halo_r, core_s, core_r, ret_s, ret_r, back_s, back_r, red_s, red_r,
+    grads, half, got1, mid1, got2, mid2, got3,
+    mine, back_out, total, ret_out, ret_in, local,
+    load_s, halo_s, halo_r, core_s, core_r, ret_s, ret_r, back_s, back_r, half_s, half_r, red_s, red_r,
 ):
     y, px, z, tp = place()
     lat, lon = lax.axis_index("lat"), lax.axis_index("lon")
@@ -93,8 +94,16 @@
     along_y = [device_at((y + d) % 4, px, z, tp) for d in (1, 2, 3)]
     along_x = [device_at(y, (px + d) % 4, z, tp) for d in (1, 2, 3)]
     along_z = [device_at(y, px, (z + d) % 4, tp) for d in (1, 2, 3)]
-    to_a, to_c, to_b = (lat, before, tp), (1 - lat, before, tp), (1 - lat, lon, tp)
+    to_a, to_b, to_c = (lat, before, tp), (1 - lat, lon, tp), (1 - lat, before, tp)
     from_a, from_c = (lat, after, tp), (1 - lat, after, tp)
+
+    pairs = (
+        (x_h, x), (send_mh, send_m), (g_h, g), (own_mh, own_m), (rest_mh, rest_m), (wq_h, wq), (wo_h, wo),
+        (cols_mh, cols_m), (send_th, send_t), (own_th, own_t), (cols_th, cols_t), (rest_th, rest_t),
+    )
+    loads = [pltpu.make_async_copy(a, b, load_s.at[i]) for i, (a, b) in enumerate(pairs)]
+    for c in loads:
+        c.start()
 
     barrier = pltpu.get_barrier_semaphore()
     greeted = [other, to_a, to_c, from_a, from_c] + along_y + along_x + along_z
@@ -105,6 +114,8 @@
         return pltpu.make_async_remote_copy(
             src_ref=src, dst_ref=dst, send_sem=s, recv_sem=r, device_id=peer, device_id_type=MESH
         )
+
+    loads[0].wait()
 
     @pl.loop(0, OWN // 64)
     def _(i):
@@ -118,12 +129,15 @@
         nat[rows, :D] = (v * s).astype(bf16)
         nat[rows, D:] = mask[rows, :]
 
+    for c in loads[1:5]:
+        c.wait()
+    out_g[...] = dot(send_m[...], g[...]).astype(bf16)
     out_n[...] = dot(send_m[...], nat[...]).astype(bf16)
-    out_g[...] = dot(send_m[...], g[...]).astype(bf16)
     pl.semaphore_wait(barrier, len(greeted))
 
     halos = []
-    for i, ((start, size), peer) in enumerate(zip(PARTS, (to_a, to_c, to_b))):
+    for i, peer in ((1, to_b), (0, to_a), (2, to_c)):
+        start, size = PARTS[i]
         rows = pl.ds(start, size)
         halos.append(copy(out_n.at[rows], in_n.at[rows], halo_s.at[0, i], halo_r.at[0, i], peer))
         halos.append(copy(out_g.at[rows], in_g.at[rows], halo_s.at[1, i], halo_r.at[1, i], peer))
@@ -136,12 +150,19 @@
             copy(gw.at[tp, w], gw.at[tp, w], core_s.at[1, w], core_r.at[1, w], other),
         )
 
+    def borrowed(w):
+        if w == 3:
+            return [(rest_m[0, :, :B_ROWS], A_ROWS, B_ROWS)]
+        if w == 7:
+            return [(cols_m[3], 0, A_ROWS), (rest_m[1], A_ROWS, BC_ROWS)]
+        return [(cols_m[w - 4], 0, A_ROWS)] if w > 3 else []
+
     def assemble(w):
         rows = pl.ds(BAND_START[w % 4], 160)
         n, c = dot(own_m[own_kind(w)], nat[rows, :]), dot(own_m[own_kind(w)], g[rows, :])
-        if w >= LOCAL:
-            n += dot(halo_m[w - LOCAL], in_n[...])
-            c += dot(halo_m[w - LOCAL], in_g[...])
+        for pick, start, size in borrowed(w):
+            n += dot(pick, in_n[start : start + size])
+            c += dot(pick, in_g[start : start + size])
         nw[tp, w] = n.astype(bf16)
         gw[tp, w] = c.astype(bf16)
         for e in exchanges(w):
@@ -163,8 +184,8 @@
         open_key = jnp.where(t == s, 1.0, keys)
         bias[w] = jnp.where((open_key == 1.0) & (crossing == 0), 0.0, -1e30)
 
-    def project(p, start, size):
-        rows, c = pl.ds(start, size), pl.ds(p * GROUP, GROUP)
+    def project(p, w, count=1):
+        rows, c = pl.ds(pl.multiple_of(w * SEQ, 16), count * SEQ), pl.ds(p * GROUP, GROUP)
         n = nf[rows, :]
         for j in range(3):
             o = dot(n, wq[j, :, c]).astype(bf16)
@@ -202,11 +223,19 @@
     first, second = (y, px), (px, y)
     peers = ((along_y, along_x), (along_x, along_y))
 
+    def halves(p, color, d):
+        side = (1, 3).index(d)
+        return copy(
+            grads.at[p, color, (first[color] + 2) % 4, pl.ds(2 * side, 2)],
+            half.at[p, color, side],
+            half_s.at[p, color, side], half_r.at[p, color, side], peers[color][0][d - 1],
+        )
+
     def stage(n, p, color, d):
         sems = (red_s.at[p, color, n, d - 1], red_r.at[p, color, n, d - 1])
         if n == 0:
             src = grads.at[p, color, (first[color] + d) % 4]
-            return copy(src, got1.at[p, color, d - 1], *sems, peers[color][0][d - 1])
+            return copy(src, got1.at[p, color, d // 2], *sems, peers[color][0][d - 1])
         if n == 1:
             src = mid1.at[p, color, (second[color] + d) % 4]
             return copy(src, got2.at[p, color, d - 1], *sems, peers[color][1][d - 1])
@@ -215,7 +244,7 @@
 
     def weight_grads(p):
         c = pl.ds(p * GROUP, GROUP)
-        for d in (1, 2, 3, 0):
+        for d in (2, 1, 3, 0):
             row = (y + d) % 4
             a = n_t[pl.ds(pl.multiple_of(row * 256, 256), 256), :]
             col = (px + d) % 4
@@ -231,19 +260,31 @@
                 val = val.astype(bf16)
                 for i in range(4):
                     grads[p, color, (row, col)[color], i, m] = val[64 * i : 64 * i + 64]
-            if d:
-                stage(0, p, 0, d).start()
-                stage(0, p, 1, d).start()
+            if d == 2:
+                for color in (0, 1):
+                    for side in (1, 3):
+                        halves(p, color, side).start()
+
+    def reduce_near(p):
+        for color in (0, 1):
+            for d in (1, 3):
+                side = d // 2
+                halves(p, color, d).wait_recv()
+                to = (first[color] + d) % 4
+                for i in range(2 * side, 2 * side + 2):
+                    s = grads[p, color, to, i].astype(f32) + half[p, color, side, i - 2 * side].astype(f32)
+                    grads[p, color, to, i] = s.astype(bf16)
+                stage(0, p, color, d).start()
 
     def reduce_first(p):
         for color in (0, 1):
-            for d in (1, 2, 3):
+            for d in (1, 3):
                 stage(0, p, color, d).wait_recv()
 
             @pl.loop(0, 4)
             def _(i):
                 s = grads[p, color, first[color], i].astype(f32)
-                for d in range(3):
+                for d in range(2):
                     s += got1[p, color, d, i].astype(f32)
                 mid1[p, color, i] = s.astype(bf16)
 
@@ -272,68 +313,95 @@
             for i in range(1, 4):
                 s += got3[p, i, color].astype(f32)
             for m in range(2):
-                dw[2 * color + m, :, p * GROUP : p * GROUP + GROUP] = s[m]
-
-    for w in range(LOCAL):
-        assemble(w)
-    pl.loop(0, LOCAL)(gather)
-    for p in range(PASSES):
-        project(p, 0, LOCAL * SEQ)
-        pl.loop(0, LOCAL)(lambda w, p=p: attend(p, w))
-    for c in halos:
-        c.wait_recv()
-    for w in range(LOCAL, WINDOWS):
-        assemble(w)
-    pl.loop(LOCAL, WINDOWS)(gather)
-    for i in range(9):
+                to = dwo if color and m else dwq.at[2 * color + m]
+                to[:, p * GROUP : p * GROUP + GROUP] = s[m]
+
+    def returned(w):
+        return copy(back_out.at[w], total.at[w], back_s.at[w], back_r.at[w], other)
+
+    def d_normed(first):
+        rows = pl.ds(first * SEQ, 2 * SEQ)
+        o = sum(dot(dp[j, rows, :], wq[j], NT) for j in range(3))
+        pad = jnp.zeros((SLOT - LEVEL, D), f32)
+        for w in (first, first + 1):
+            v = o[(w - first) * SEQ : (w - first + 1) * SEQ]
+            lo, hi = jnp.concatenate([v[:LEVEL], pad]), jnp.concatenate([v[LEVEL:], pad])
+            mine[w] = jnp.where(tp == 0, lo, hi)
+            back_out[w] = jnp.where(tp == 0, hi, lo).astype(bf16)
+            returned(w).start()
+
+    def add(w):
+        returned(w).wait_recv()
+        total[w] = (mine[w] + total[w].astype(f32)).astype(bf16)
+
+    def transposed(i):
         rows = pl.ds(i * 128, 128)
         n_t[:, i * 128 : i * 128 + 128] = nf[rows, :].T
         g_t[:, i * 128 : i * 128 + 128] = gf[rows, :].T
+
+    for w in range(EARLY - 1):
+        assemble(w)
+    pl.loop(0, EARLY - 1)(gather)
+    for c in loads[5:]:
+        c.wait()
+    project(0, 0, 3)
+    pl.loop(0, 3)(lambda w: attend(0, w))
+    for c in halos[:2]:
+        c.wait_recv()
+    assemble(3)
+    project(1, 0, 3)
+    pl.loop(0, 3)(lambda w: attend(1, w))
+    gather(jnp.int32(3))
     for p in range(PASSES):
-        project(p, LOCAL * SEQ, (WINDOWS - LOCAL) * SEQ)
-        pl.loop(LOCAL, WINDOWS)(lambda w, p=p: attend(p, w))
-        if p:
-            reduce_first(p - 1)
-        weight_grads(p)
-        if p:
-            reduce_second(p - 1)
-
-    def returned(w):
-        return copy(back_out.at[w], back_in.at[w], back_s.at[w], back_r.at[w], other)
-
-    def d_normed(w):
-        rows = pl.ds(pl.multiple_of(w * SEQ, 16), SEQ)
-        o = sum(dot(dp[j, rows, :], wq[j], NT) for j in range(3))
-        pad = jnp.zeros((SLOT - LEVEL, D), f32)
-        lo, hi = jnp.concatenate([o[:LEVEL], pad]), jnp.concatenate([o[LEVEL:], pad])
-        mine[w] = jnp.where(tp == 0, lo, hi)
-        back_out[w] = jnp.where(tp == 0, hi, lo).astype(bf16)
-        returned(w).start()
-
-    pl.loop(LOCAL, WINDOWS)(d_normed)
-    pl.loop(0, LOCAL)(d_normed)
-    reduce_first(PASSES - 1)
-
-    def add(w):
-        returned(w).wait_recv()
-        total[w] = (mine[w] + back_in[w].astype(f32)).astype(bf16)
-
-    pl.loop(LOCAL, WINDOWS)(add)
-    ret_out[...] = sum(dot(halo_t[w - LOCAL], total[w]) for w in range(LOCAL, WINDOWS)).astype(bf16)
+        project(p, 3)
+        attend(p, 3)
+    for w in (0, 2):
+        d_normed(w)
+    for i in range(4):
+        transposed(i)
+    pl.loop(0, EARLY)(add)
+    for c in halos[2:]:
+        c.wait_recv()
+    for w in range(EARLY, WINDOWS):
+        assemble(w)
+
+    @pl.loop(EARLY, WINDOWS)
+    def _(w):
+        gather(w)
+        project(0, w)
+        attend(0, w)
+
+    for i in range(4, 9):
+        transposed(i)
+    weight_grads(0)
+    project(1, EARLY, WINDOWS - EARLY)
+    reduce_near(0)
+    pl.loop(EARLY, WINDOWS)(lambda w: attend(1, w))
+    weight_grads(1)
+    for w in (4, 6):
+        d_normed(w)
+    reduce_first(0)
+    reduce_near(1)
+    pl.loop(EARLY, WINDOWS)(add)
+    ret_out[:A_ROWS] = sum(dot(cols_t[b], total[4 + b]) for b in range(4)).astype(bf16)
+    ret_out[A_ROWS:] = sum(dot(rest_t[j], total[3 + 4 * j]) for j in range(2)).astype(bf16)
     returns = []
-    for i, ((start, size), peer) in enumerate(zip(PARTS, (from_a, from_c, to_b))):
+    for i, peer in enumerate((from_a, to_b, from_c)):
+        start, size = PARTS[i]
         rows = pl.ds(start, size)
         returns.append(copy(ret_out.at[rows], ret_in.at[rows], ret_s.at[i], ret_r.at[i], peer))
     for c in returns:
         c.start()
-    pl.loop(0, LOCAL)(add)
     local[:LEVEL] = jnp.zeros((LEVEL, D), f32)
     for b in range(4):
         o = dot(own_t[own_kind(b)], total[b]) + dot(own_t[own_kind(b + 4)], total[b + 4])
         skip = 72 + 144 * b - BAND_START[b]
         size = 144 if b < 3 else 72
         local[72 + 144 * b : 72 + 144 * b + size] = o[skip : skip + size]
-    reduce_second(PASSES - 1)
+    reduce_second(0)
+    reduce_first(1)
+    reduce_third(0)
+    reduce_second(1)
     for c in returns:
         c.wait_recv()
 
@@ -346,8 +414,7 @@
         inner = dn - jnp.mean(dn, axis=-1, keepdims=True) - xh * jnp.mean(dn * xh, axis=-1, keepdims=True)
         dtok[rows, :] = (s * inner + g[rows, :].astype(f32)).astype(bf16)
 
-    for p in range(PASSES):
-        reduce_third(p)
+    reduce_third(1)
     for c in halos + returns:
         c.wait_send()
 
@@ -358,10 +425,13 @@
         returned(w).wait_send()
 
     for p in range(PASSES):
-        for n in range(3):
-            for color in (0, 1):
-                for d in (1, 2, 3):
-                    stage(n, p, color, d).wait_send()
+        for color in (0, 1):
+            for d in (1, 2, 3):
+                if d != 2:
+                    halves(p, color, d).wait_send()
+                    stage(0, p, color, d).wait_send()
+                stage(1, p, color, d).wait_send()
+                stage(2, p, color, d).wait_send()
 
 
 def body(tokens, land_mask, qkv_weight, out_weight, out_grad):
@@ -370,12 +440,18 @@
     operands = [tokens.reshape(OWN, D), out_grad.reshape(OWN, D), mask, qkv_weight, out_weight] + constants
     vmem, dma = pltpu.VMEM, pltpu.SemaphoreType.DMA
     tokens_all = WINDOWS * SEQ
-    d_tokens, d_weights = pl.pallas_call(
+    in_place = [a for i, a in enumerate(operands) if i != 2]
+    d_tokens, d_qkv_weight, d_out_weight = pl.pallas_call(
         kernel,
-        out_shape=(jax.ShapeDtypeStruct((OWN, D), bf16), jax.ShapeDtypeStruct((4, 32, 512), f32)),
-        in_specs=[pl.BlockSpec(memory_space=pltpu.VMEM)] * len(operands),
-        out_specs=[pl.BlockSpec(memory_space=pltpu.VMEM)] * 2,
-        scratch_shapes=[
+        out_shape=(
+            jax.ShapeDtypeStruct((OWN, D), bf16),
+            jax.ShapeDtypeStruct((3, 32, 512), f32),
+            jax.ShapeDtypeStruct((32, 512), f32),
+        ),
+        in_specs=[pl.BlockSpec(memory_space=pltpu.VMEM if i == 2 else pl.ANY) for i in range(len(operands))],
+        out_specs=[pl.BlockSpec(memory_space=pltpu.VMEM)] * 3,
+        scratch_shapes=[vmem(a.shape, bf16) for a in in_place]
+        + [
             vmem((OWN, WIDE), bf16),
             vmem((OWN, 1), f32),
             vmem((OWN, 1), f32),
@@ -395,7 +471,8 @@
             vmem((tokens_all, 512), bf16),
             vmem((3, tokens_all, 512), bf16),
             vmem((PASSES, 2, 4, 4, 2, 64, GROUP), bf16),
-            vmem((PASSES, 2, 3, 4, 2, 64, GROUP), bf16),
+            vmem((PASSES, 2, 2, 2, 2, 64, GROUP), bf16),
+            vmem((PASSES, 2, 2, 4, 2, 64, GROUP), bf16),
             vmem((PASSES, 2, 4, 2, 64, GROUP), bf16),
             vmem((PASSES, 2, 3, 2, 64, GROUP), bf16),
             vmem((PASSES, 2, 2, 2, 32, GROUP), bf16),
@@ -403,10 +480,10 @@
             vmem((WINDOWS, SLOT, D), f32),
             vmem((WINDOWS, SLOT, D), bf16),
             vmem((WINDOWS, SLOT, D), bf16),
-            vmem((WINDOWS, SLOT, D), bf16),
             vmem((HALO, D), bf16),
             vmem((HALO, D), bf16),
             vmem((OWN, D), f32),
+            dma((len(in_place),)),
             dma((2, 3)),
             dma((2, 3)),
             dma((2, WINDOWS)),
@@ -415,6 +492,8 @@
             dma((3,)),
             dma((WINDOWS,)),
             dma((WINDOWS,)),
+            dma((PASSES, 2, 2)),
+            dma((PASSES, 2, 2)),
             dma((PASSES, 2, 3, 3)),
             dma((PASSES, 2, 3, 3)),
         ],
@@ -423,7 +502,7 @@
         ),
         name="swin_backward",
     )(*operands)
-    return d_tokens.reshape(ROWS, COLS, 1, D), d_weights[:3], d_weights[3].T
+    return d_tokens.reshape(ROWS, COLS, 1, D), d_qkv_weight, d_out_weight.T
 
 
 def solution(mesh):

time: 100 us -> 89.6 us (0.90)
  Pallas kernels: 91.7 us -> 83.4 us
  local copies, waits for them, and re-layouts: 6.36 us -> 4.63 us
    pallas_call x1, Pallas kernels: 91.7 us -> 83.4 us  [body(): pl.pallas_call(kernel, out_shape=(jax.ShapeDtypeStruct((OWN, D), bf16), j...]
    slice x1 -> x0, local copies, waits for them, and re-layouts: 1.62 us -> none  [body(): return (d_tokens.reshape(ROWS, COLS, 1, D), d_weights[:3], d_weights[3].T)]
    transpose x1 -> x0, local copies, waits for them, and re-layouts: 1.47 us -> none  [body(): return (d_tokens.reshape(ROWS, COLS, 1, D), d_weights[:3], d_weights[3].T)]
    unnamed x1 -> x7, local copies, waits for them, and re-layouts: 2.37 us -> 3.72 us
where the time goes in v3:
time: 89.6 us; the launch traced here: 89.4 us
  Pallas kernels  83.4 us (93%)
  local copies, waits for them, and re-layouts  4.63 us (5%)
    pallas_call x1, Pallas kernels, body(): pl.pallas_call(kernel, out_shape=(jax.ShapeDtypeStruct((OWN, D), bf16), j...  83.4 us
    unnamed x7, local copies, waits for them, and re-layouts  3.72 us

profile of v3, /device:TPU:0, one launch (start us, length us, event | category | flops | bytes accessed | tf_op | source)
XLA Modules:
  0.0 89.4 jit_solution(1303499666424399280)
XLA Ops:
  0.6 0.8 convert_reduce_fusion
  1.4 0.1 convert_element_type.12
  1.5 0.8 broadcast_in_dim.2.mask
  2.3 83.4 %swin_backward.1 = (bf16[576,1024]{1,0:T(8,128)(2,1)}, f32[3,32,512]{2,1,0:T(8,128)}, f32[32,512]{1,0:T(8,128)}) custom-call(bf16[576,1024]{1,0:T(8,128)(2,1)} %bitcast.7, bf16[576,1024]{1,0:T(8,128)(2,1)} %bitcast.8, bf16[576,128]{1,0:T(8,128)(2,1)} %broadcast_in_dim.2.mask, bf16[3,1024,512]{2,1,0:T(8,128)(2,1)} %wq_h.1, bf16[512,1024]{1,0:T(8,128)(2,1)} %wo_h.1, ...), custom_call_target="tpu_custom_call" | custom-call | tf_op jit(solution)/shard_map/swin_backward/pallas_call | solution.py:444
  85.7 0.0 copy-start
  85.7 0.0 copy-start.1
  85.7 2.4 %copy.20 = bf16[24,24,1,1024]{3,1,2,0:T(8,128)(2,1)} copy(bf16[24,24,1,1024]{3,1,2,0:T(8,128)(2,1)} %bitcast.6) | data formatting | bytes 2359296
  88.1 0.0 copy-done
  88.1 0.7 copy.21
  88.8 0.0 copy-done.1
  88.8 0.6 copy.22
Async XLA Ops:
  85.7 2.4 %copy-start = (f32[3,32,512]{2,1,0:T(8,128)S(1)}, f32[3,32,512]{2,1,0:T(8,128)}, u32[]{:S(2)}) copy-start(f32[3,32,512]{2,1,0:T(8,128)} %get-tuple-element.16) | copy-start | bytes 589828
  85.7 3.1 %copy-start.1 = (f32[32,512]{1,0:T(8,128)S(1)}, f32[32,512]{1,0:T(8,128)}, u32[]{:S(2)}) copy-start(f32[32,512]{1,0:T(8,128)} %get-tuple-element.8) | copy-start | bytes 196612

commit v4 on v3

--- a/solution.py
+++ b/solution.py
@@ -58,7 +58,10 @@
                         rest[j, t, B_ROWS + (r - 21) * 6 + col - 18] = 1
     own = own[[0, 3, 4, 7]]
     swap = lambda a: np.ascontiguousarray(np.swapaxes(a, -1, -2))
-    return [a.astype(jnp.bfloat16) for a in (send, swap(send), own, swap(own), cols, swap(cols), rest, swap(rest))]
+    row, col = np.zeros((OWN, ROWS), np.float32), np.zeros((OWN, COLS), np.float32)
+    row[np.arange(OWN), np.arange(OWN) // COLS] = 1
+    col[np.arange(OWN), np.arange(OWN) % COLS] = 1
+    return [a.astype(jnp.bfloat16) for a in (row, col, send, swap(send), own, swap(own), cols, swap(cols), rest, swap(rest))]
 
 
 def own_kind(w):
@@ -79,9 +82,9 @@
 
 
 def kernel(
-    x_h, g_h, mask, wq_h, wo_h, send_mh, send_th, own_mh, own_th, cols_mh, cols_th, rest_mh, rest_th,
+    x_h, g_h, mask, wq_h, wo_h, row_mh, col_mh, send_mh, send_th, own_mh, own_th, cols_mh, cols_th, rest_mh, rest_th,
     dtok, dwq, dwo,
-    x, g, wq, wo, send_m, send_t, own_m, own_t, cols_m, cols_t, rest_m, rest_t,
+    x, g, wq, wo, row_m, col_m, send_m, send_t, own_m, own_t, cols_m, cols_t, rest_m, rest_t,
     nat, mean, rstd, out_n, out_g, in_n, in_g, nw, gw, nf, gf, n_t, g_t, bias, qkv, da, att, dp,
     grads, half, got1, mid1, got2, mid2, got3,
     mine, back_out, total, ret_out, ret_in, local,
@@ -98,8 +101,8 @@
     from_a, from_c = (lat, after, tp), (1 - lat, after, tp)
 
     pairs = (
-        (x_h, x), (send_mh, send_m), (g_h, g), (own_mh, own_m), (rest_mh, rest_m), (wq_h, wq), (wo_h, wo),
-        (cols_mh, cols_m), (send_th, send_t), (own_th, own_t), (cols_th, cols_t), (rest_th, rest_t),
+        (g_h, g), (send_mh, send_m), (x_h, x), (row_mh, row_m), (col_mh, col_m), (own_mh, own_m), (wq_h, wq), (wo_h, wo),
+        (rest_mh, rest_m), (cols_mh, cols_m), (send_th, send_t), (own_th, own_t), (cols_th, cols_t), (rest_th, rest_t),
     )
     loads = [pltpu.make_async_copy(a, b, load_s.at[i]) for i, (a, b) in enumerate(pairs)]
     for c in loads:
@@ -115,7 +118,24 @@
             src_ref=src, dst_ref=dst, send_sem=s, recv_sem=r, device_id=peer, device_id_type=MESH
         )
 
-    loads[0].wait()
+    halos = [[], []]
+    for i, peer in ((1, to_b), (0, to_a), (2, to_c)):
+        start, size = PARTS[i]
+        rows = pl.ds(start, size)
+        halos[0].append(copy(out_g.at[rows], in_g.at[rows], halo_s.at[0, i], halo_r.at[0, i], peer))
+        halos[1].append(copy(out_n.at[rows], in_n.at[rows], halo_s.at[1, i], halo_r.at[1, i], peer))
+    for c in loads[:2]:
+        c.wait()
+    out_g[...] = dot(send_m[...], g[...]).astype(bf16)
+    pl.semaphore_wait(barrier, len(greeted))
+    for c in halos[0]:
+        c.start()
+
+    for c in loads[2:6]:
+        c.wait()
+    open_rows = jnp.concatenate([mask[r].astype(f32) for r in range(ROWS)]).astype(bf16)
+    open_own = jnp.sum(dot(row_m[...], open_rows) * col_m[...].astype(f32), axis=-1, keepdims=True)
+    nat[:, D:] = jnp.broadcast_to(open_own, (OWN, 128)).astype(bf16)
 
     @pl.loop(0, OWN // 64)
     def _(i):
@@ -127,22 +147,9 @@
         mean[rows, :] = m
         rstd[rows, :] = s
         nat[rows, :D] = (v * s).astype(bf16)
-        nat[rows, D:] = mask[rows, :]
-
-    for c in loads[1:5]:
-        c.wait()
-    out_g[...] = dot(send_m[...], g[...]).astype(bf16)
+
     out_n[...] = dot(send_m[...], nat[...]).astype(bf16)
-    pl.semaphore_wait(barrier, len(greeted))
-
-    halos = []
-    for i, peer in ((1, to_b), (0, to_a), (2, to_c)):
-        start, size = PARTS[i]
-        rows = pl.ds(start, size)
-        halos.append(copy(out_n.at[rows], in_n.at[rows], halo_s.at[0, i], halo_r.at[0, i], peer))
-        halos.append(copy(out_g.at[rows], in_g.at[rows], halo_s.at[1, i], halo_r.at[1, i], peer))
-    for c in halos:
-        c.start()
+    halos[1][0].start()
 
     def exchanges(w):
         return (
@@ -186,10 +193,10 @@
 
     def project(p, w, count=1):
         rows, c = pl.ds(pl.multiple_of(w * SEQ, 16), count * SEQ), pl.ds(p * GROUP, GROUP)
-        n = nf[rows, :]
+        o = dot(nf[rows, :], jnp.concatenate([wq[j, :, c] for j in range(3)], axis=1)).astype(bf16)
         for j in range(3):
-            o = dot(n, wq[j, :, c]).astype(bf16)
-            qkv[j, rows, :] = o * bf16(0.125) if j == 0 else o
+            part = o[:, j * GROUP : (j + 1) * GROUP]
+            qkv[j, rows, :] = part * bf16(0.125) if j == 0 else part
         da[rows, :] = dot(gf[rows, :], wo[c, :], NT).astype(bf16)
 
     lane = lax.broadcasted_iota(jnp.int32, (1, GROUP), 1) // 64
@@ -223,24 +230,24 @@
     first, second = (y, px), (px, y)
     peers = ((along_y, along_x), (along_x, along_y))
 
-    def halves(p, color, d):
+    def halves(p, color, d, m):
         side = (1, 3).index(d)
         return copy(
-            grads.at[p, color, (first[color] + 2) % 4, pl.ds(2 * side, 2)],
-            half.at[p, color, side],
-            half_s.at[p, color, side], half_r.at[p, color, side], peers[color][0][d - 1],
+            grads.at[p, color, m, (first[color] + 2) % 4, pl.ds(2 * side, 2)],
+            half.at[p, color, m, side],
+            half_s.at[p, color, m, side], half_r.at[p, color, m, side], peers[color][0][d - 1],
         )
 
-    def stage(n, p, color, d):
-        sems = (red_s.at[p, color, n, d - 1], red_r.at[p, color, n, d - 1])
+    def stage(n, p, color, d, m):
+        sems = (red_s.at[p, color, m, n, d - 1], red_r.at[p, color, m, n, d - 1])
         if n == 0:
-            src = grads.at[p, color, (first[color] + d) % 4]
-            return copy(src, got1.at[p, color, d // 2], *sems, peers[color][0][d - 1])
+            src = grads.at[p, color, m, (first[color] + d) % 4]
+            return copy(src, got1.at[p, color, m, d // 2], *sems, peers[color][0][d - 1])
         if n == 1:
-            src = mid1.at[p, color, (second[color] + d) % 4]
-            return copy(src, got2.at[p, color, d - 1], *sems, peers[color][1][d - 1])
-        src = mid2.at[p, color, ((z + d) % 4) // 2]
-        return copy(src, got3.at[p, z, color], *sems, along_z[d - 1])
+            src = mid1.at[p, color, m, (second[color] + d) % 4]
+            return copy(src, got2.at[p, color, m, d - 1], *sems, peers[color][1][d - 1])
+        src = mid2.at[p, color, m, ((z + d) % 4) // 2]
+        return copy(src, got3.at[p, z, color, m], *sems, along_z[d - 1])
 
     def weight_grads(p):
         c = pl.ds(p * GROUP, GROUP)
@@ -251,70 +258,66 @@
             pieces = [pl.ds(pl.multiple_of(i * 256 + col * 64, 64), 64) for i in range(4)]
             b = jnp.concatenate([n_t[i, :] for i in pieces])
             e = jnp.concatenate([g_t[i, :] for i in pieces])
+            near = dot(a, jnp.concatenate([dp[0, :, c], dp[1, :, c]], axis=1))
             for color, m, val in (
-                (0, 0, dot(a, dp[0, :, c])),
-                (0, 1, dot(a, dp[1, :, c])),
+                (0, 0, near[:, :GROUP]),
+                (0, 1, near[:, GROUP:]),
                 (1, 0, dot(b, dp[2, :, c])),
                 (1, 1, dot(e, att[:, c])),
             ):
                 val = val.astype(bf16)
                 for i in range(4):
-                    grads[p, color, (row, col)[color], i, m] = val[64 * i : 64 * i + 64]
-            if d == 2:
-                for color in (0, 1):
+                    grads[p, color, m, (row, col)[color], i] = val[64 * i : 64 * i + 64]
+                if d == 2:
                     for side in (1, 3):
-                        halves(p, color, side).start()
+                        halves(p, color, side, m).start()
+
+    both = [(color, m) for m in range(2) for color in range(2)]
 
     def reduce_near(p):
-        for color in (0, 1):
+        for color, m in both:
             for d in (1, 3):
                 side = d // 2
-                halves(p, color, d).wait_recv()
-                to = (first[color] + d) % 4
-                for i in range(2 * side, 2 * side + 2):
-                    s = grads[p, color, to, i].astype(f32) + half[p, color, side, i - 2 * side].astype(f32)
-                    grads[p, color, to, i] = s.astype(bf16)
-                stage(0, p, color, d).start()
+                halves(p, color, d, m).wait_recv()
+                to, rows = (first[color] + d) % 4, pl.ds(2 * side, 2)
+                s = grads[p, color, m, to, rows].astype(f32) + half[p, color, m, side].astype(f32)
+                grads[p, color, m, to, rows] = s.astype(bf16)
+                stage(0, p, color, d, m).start()
 
     def reduce_first(p):
-        for color in (0, 1):
+        for color, m in both:
             for d in (1, 3):
-                stage(0, p, color, d).wait_recv()
-
-            @pl.loop(0, 4)
-            def _(i):
-                s = grads[p, color, first[color], i].astype(f32)
-                for d in range(2):
-                    s += got1[p, color, d, i].astype(f32)
-                mid1[p, color, i] = s.astype(bf16)
-
+                stage(0, p, color, d, m).wait_recv()
+            s = grads[p, color, m, first[color]].astype(f32)
+            for d in range(2):
+                s += got1[p, color, m, d].astype(f32)
+            mid1[p, color, m] = s.astype(bf16)
             for d in (1, 2, 3):
-                stage(1, p, color, d).start()
+                stage(1, p, color, d, m).start()
 
     def reduce_second(p):
-        for color in (0, 1):
+        for color, m in both:
             for d in (1, 2, 3):
-                stage(1, p, color, d).wait_recv()
-            s = mid1[p, color, second[color]].astype(f32)
+                stage(1, p, color, d, m).wait_recv()
+            s = mid1[p, color, m, second[color]].astype(f32)
             for d in range(3):
-                s += got2[p, color, d].astype(f32)
+                s += got2[p, color, m, d].astype(f32)
             s = s.astype(bf16)
-            mid2[p, color, 0] = s[:, :32]
-            mid2[p, color, 1] = s[:, 32:]
-            got3[p, z, color] = mid2[p, color, z // 2]
+            mid2[p, color, m, 0] = s[:32]
+            mid2[p, color, m, 1] = s[32:]
+            got3[p, z, color, m] = mid2[p, color, m, z // 2]
             for d in (1, 2, 3):
-                stage(2, p, color, d).start()
+                stage(2, p, color, d, m).start()
 
     def reduce_third(p):
-        for color in (0, 1):
+        for color, m in both:
             for d in (1, 2, 3):
-                stage(2, p, color, d).wait_recv()
-            s = got3[p, 0, color].astype(f32)
+                stage(2, p, color, d, m).wait_recv()
+            s = got3[p, 0, color, m].astype(f32)
             for i in range(1, 4):
-                s += got3[p, i, color].astype(f32)
-            for m in range(2):
-                to = dwo if color and m else dwq.at[2 * color + m]
-                to[:, p * GROUP : p * GROUP + GROUP] = s[m]
+                s += got3[p, i, color, m].astype(f32)
+            to = dwo if color and m else dwq.at[2 * color + m]
+            to[:, p * GROUP : p * GROUP + GROUP] = s
 
     def returned(w):
         return copy(back_out.at[w], total.at[w], back_s.at[w], back_r.at[w], other)
@@ -342,25 +345,27 @@
     for w in range(EARLY - 1):
         assemble(w)
     pl.loop(0, EARLY - 1)(gather)
-    for c in loads[5:]:
+    for c in halos[1][1:]:
+        c.start()
+    for c in loads[6:]:
         c.wait()
-    project(0, 0, 3)
-    pl.loop(0, 3)(lambda w: attend(0, w))
-    for c in halos[:2]:
+    for p in range(PASSES):
+        project(p, 0, EARLY - 1)
+        pl.loop(0, EARLY - 1)(lambda w, p=p: attend(p, w))
+    for c in halos[0][:1] + halos[1][:1]:
         c.wait_recv()
     assemble(3)
-    project(1, 0, 3)
-    pl.loop(0, 3)(lambda w: attend(1, w))
+    d_normed(0)
+    for i in range(3):
+        transposed(i)
     gather(jnp.int32(3))
     for p in range(PASSES):
         project(p, 3)
         attend(p, 3)
-    for w in (0, 2):
-        d_normed(w)
-    for i in range(4):
-        transposed(i)
+    d_normed(2)
+    transposed(3)
     pl.loop(0, EARLY)(add)
-    for c in halos[2:]:
+    for c in halos[0][1:] + halos[1][1:]:
         c.wait_recv()
     for w in range(EARLY, WINDOWS):
         assemble(w)
@@ -374,14 +379,22 @@
     for i in range(4, 9):
         transposed(i)
     weight_grads(0)
-    project(1, EARLY, WINDOWS - EARLY)
-    reduce_near(0)
-    pl.loop(EARLY, WINDOWS)(lambda w: attend(1, w))
-    weight_grads(1)
-    for w in (4, 6):
-        d_normed(w)
-    reduce_first(0)
-    reduce_near(1)
+    for p in range(1, PASSES):
+        project(p, EARLY, WINDOWS - EARLY)
+        reduce_near(p - 1)
+        if p > 1:
+            reduce_first(p - 2)
+        pl.loop(EARLY, WINDOWS)(lambda w, p=p: attend(p, w))
+        if p > 2:
+            reduce_second(p - 3)
+        weight_grads(p)
+    last = PASSES - 1
+    d_normed(4)
+    d_normed(6)
+    reduce_near(last)
+    reduce_first(last - 1)
+    if last > 1:
+        reduce_second(last - 2)
     pl.loop(EARLY, WINDOWS)(add)
     ret_out[:A_ROWS] = sum(dot(cols_t[b], total[4 + b]) for b in range(4)).astype(bf16)
     ret_out[A_ROWS:] = sum(dot(rest_t[j], total[3 + 4 * j]) for j in range(2)).astype(bf16)
@@ -398,10 +411,10 @@
         skip = 72 + 144 * b - BAND_START[b]
         size = 144 if b < 3 else 72
         local[72 + 144 * b : 72 + 144 * b + size] = o[skip : skip + size]
-    reduce_second(0)
-    reduce_first(1)
-    reduce_third(0)
-    reduce_second(1)
+    for p in range(last - 1):
+        reduce_third(p)
+    reduce_second(last - 1)
+    reduce_first(last)
     for c in returns:
         c.wait_recv()
 
@@ -414,8 +427,10 @@
         inner = dn - jnp.mean(dn, axis=-1, keepdims=True) - xh * jnp.mean(dn * xh, axis=-1, keepdims=True)
         dtok[rows, :] = (s * inner + g[rows, :].astype(f32)).astype(bf16)
 
-    reduce_third(1)
-    for c in halos + returns:
+    reduce_third(last - 1)
+    reduce_second(last)
+    reduce_third(last)
+    for c in halos[0] + halos[1] + returns:
         c.wait_send()
 
     @pl.loop(0, WINDOWS)
@@ -425,17 +440,17 @@
         returned(w).wait_send()
 
     for p in range(PASSES):
-        for color in (0, 1):
+        for color, m in both:
             for d in (1, 2, 3):
                 if d != 2:
-                    halves(p, color, d).wait_send()
-                    stage(0, p, color, d).wait_send()
-                stage(1, p, color, d).wait_send()
-                stage(2, p, color, d).wait_send()
+                    halves(p, color, d, m).wait_send()
+                    stage(0, p, color, d, m).wait_send()
+                stage(1, p, color, d, m).wait_send()
+                stage(2, p, color, d, m).wait_send()
 
 
 def body(tokens, land_mask, qkv_weight, out_weight, out_grad):
-    mask = jnp.broadcast_to(land_mask.reshape(OWN, 1).astype(bf16), (OWN, 128))
+    mask = land_mask.reshape(ROWS, 1, COLS)
     constants = [jnp.asarray(a) for a in selections()]
     operands = [tokens.reshape(OWN, D), out_grad.reshape(OWN, D), mask, qkv_weight, out_weight] + constants
     vmem, dma = pltpu.VMEM, pltpu.SemaphoreType.DMA
@@ -470,11 +485,11 @@
             vmem((tokens_all, GROUP), bf16),
             vmem((tokens_all, 512), bf16),
             vmem((3, tokens_all, 512), bf16),
-            vmem((PASSES, 2, 4, 4, 2, 64, GROUP), bf16),
+            vmem((PASSES, 2, 2, 4, 4, 64, GROUP), bf16),
             vmem((PASSES, 2, 2, 2, 2, 64, GROUP), bf16),
-            vmem((PASSES, 2, 2, 4, 2, 64, GROUP), bf16),
-            vmem((PASSES, 2, 4, 2, 64, GROUP), bf16),
-            vmem((PASSES, 2, 3, 2, 64, GROUP), bf16),
+            vmem((PASSES, 2, 2, 2, 4, 64, GROUP), bf16),
+            vmem((PASSES, 2, 2, 4, 64, GROUP), bf16),
+            vmem((PASSES, 2, 2, 3, 64, GROUP), bf16),
             vmem((PASSES, 2, 2, 2, 32, GROUP), bf16),
             vmem((PASSES, 4, 2, 2, 32, GROUP), bf16),
             vmem((WINDOWS, SLOT, D), f32),
@@ -492,10 +507,10 @@
             dma((3,)),
             dma((WINDOWS,)),
             dma((WINDOWS,)),
-            dma((PASSES, 2, 2)),
-            dma((PASSES, 2, 2)),
-            dma((PASSES, 2, 3, 3)),
-            dma((PASSES, 2, 3, 3)),
+            dma((PASSES, 2, 2, 2)),
+            dma((PASSES, 2, 2, 2)),
+            dma((PASSES, 2, 2, 3, 3)),
+            dma((PASSES, 2, 2, 3, 3)),
         ],
         compiler_params=pltpu.CompilerParams(
             collective_id=0, has_side_effects=True, vmem_limit_bytes=63 * 1024 * 1024

time: 89.6 us -> 85.1 us (0.950)
  Pallas kernels: 83.4 us -> 80.6 us
  local copies, waits for them, and re-layouts: 4.63 us -> 3.72 us
    pallas_call x1, Pallas kernels: 83.4 us -> 80.6 us  [body(): pl.pallas_call(kernel, out_shape=(jax.ShapeDtypeStruct((OWN, D), bf16), j...]
where the time goes in v4:
time: 85.1 us; the launch traced here: 84.9 us
  Pallas kernels  80.6 us (95%)
  local copies, waits for them, and re-layouts  3.72 us (4%)
    pallas_call x1, Pallas kernels, body(): pl.pallas_call(kernel, out_shape=(jax.ShapeDtypeStruct((OWN, D), bf16), j...  80.6 us
    unnamed x7, local copies, waits for them, and re-layouts  3.72 us

profile of v4, /device:TPU:0, one launch (start us, length us, event | category | flops | bytes accessed | tf_op | source)
XLA Modules:
  0.0 84.9 jit_solution(13229988742356888042)
XLA Ops:
  0.6 80.6 %swin_backward.1 = (bf16[576,1024]{1,0:T(8,128)(2,1)}, f32[3,32,512]{2,1,0:T(8,128)}, f32[32,512]{1,0:T(8,128)}) custom-call(bf16[576,1024]{1,0:T(8,128)(2,1)} %bitcast.8, bf16[576,1024]{1,0:T(8,128)(2,1)} %bitcast.9, s32[24,1,24]{2,1,0:T(1,128)} %bitcast.11, bf16[3,1024,512]{2,1,0:T(8,128)(2,1)} %wq_h.1, bf16[512,1024]{1,0:T(8,128)(2,1)} %wo_h.1, ...), custom_call_target="tpu_custom_call" | custom-call | tf_op jit(solution)/shard_map/swin_backward/pallas_call | solution.py:459
  81.2 0.0 copy-start
  81.2 0.0 copy-start.1
  81.2 2.4 %copy.22 = bf16[24,24,1,1024]{3,1,2,0:T(8,128)(2,1)} copy(bf16[24,24,1,1024]{3,1,2,0:T(8,128)(2,1)} %bitcast.7) | data formatting | bytes 2359296
  83.6 0.0 copy-done
  83.6 0.7 copy.23
  84.3 0.0 copy-done.1
  84.3 0.6 copy.24
Async XLA Ops:
  81.2 2.4 %copy-start = (f32[3,32,512]{2,1,0:T(8,128)S(1)}, f32[3,32,512]{2,1,0:T(8,128)}, u32[]{:S(2)}) copy-start(f32[3,32,512]{2,1,0:T(8,128)} %get-tuple-element.16) | copy-start | bytes 589828
  81.2 3.1 %copy-start.1 = (f32[32,512]{1,0:T(8,128)S(1)}, f32[32,512]{1,0:T(8,128)}, u32[]{:S(2)}) copy-start(f32[32,512]{1,0:T(8,128)} %get-tuple-element.8) | copy-start | bytes 196612

commit v5 on v4

--- a/solution.py
+++ b/solution.py
@@ -128,8 +128,7 @@
         c.wait()
     out_g[...] = dot(send_m[...], g[...]).astype(bf16)
     pl.semaphore_wait(barrier, len(greeted))
-    for c in halos[0]:
-        c.start()
+    halos[0][0].start()
 
     for c in loads[2:6]:
         c.wait()
@@ -345,17 +344,17 @@
     for w in range(EARLY - 1):
         assemble(w)
     pl.loop(0, EARLY - 1)(gather)
-    for c in halos[1][1:]:
+    for c in halos[0][1:] + halos[1][1:]:
         c.start()
     for c in loads[6:]:
         c.wait()
     for p in range(PASSES):
         project(p, 0, EARLY - 1)
         pl.loop(0, EARLY - 1)(lambda w, p=p: attend(p, w))
+    d_normed(0)
     for c in halos[0][:1] + halos[1][:1]:
         c.wait_recv()
     assemble(3)
-    d_normed(0)
     for i in range(3):
         transposed(i)
     gather(jnp.int32(3))
@@ -364,7 +363,6 @@
         attend(p, 3)
     d_normed(2)
     transposed(3)
-    pl.loop(0, EARLY)(add)
     for c in halos[0][1:] + halos[1][1:]:
         c.wait_recv()
     for w in range(EARLY, WINDOWS):
@@ -395,7 +393,7 @@
     reduce_first(last - 1)
     if last > 1:
         reduce_second(last - 2)
-    pl.loop(EARLY, WINDOWS)(add)
+    pl.loop(EARLY - 1, WINDOWS)(add)
     ret_out[:A_ROWS] = sum(dot(cols_t[b], total[4 + b]) for b in range(4)).astype(bf16)
     ret_out[A_ROWS:] = sum(dot(rest_t[j], total[3 + 4 * j]) for j in range(2)).astype(bf16)
     returns = []
@@ -405,6 +403,7 @@
         returns.append(copy(ret_out.at[rows], ret_in.at[rows], ret_s.at[i], ret_r.at[i], peer))
     for c in returns:
         c.start()
+    pl.loop(0, EARLY - 1)(add)
     local[:LEVEL] = jnp.zeros((LEVEL, D), f32)
     for b in range(4):
         o = dot(own_t[own_kind(b)], total[b]) + dot(own_t[own_kind(b + 4)], total[b + 4])
@@ -415,6 +414,8 @@
         reduce_third(p)
     reduce_second(last - 1)
     reduce_first(last)
+    reduce_third(last - 1)
+    reduce_second(last)
     for c in returns:
         c.wait_recv()
 
@@ -427,8 +428,6 @@
         inner = dn - jnp.mean(dn, axis=-1, keepdims=True) - xh * jnp.mean(dn * xh, axis=-1, keepdims=True)
         dtok[rows, :] = (s * inner + g[rows, :].astype(f32)).astype(bf16)
 
-    reduce_third(last - 1)
-    reduce_second(last)
     reduce_third(last)
     for c in halos[0] + halos[1] + returns:
         c.wait_send()

time: 85.1 us -> 90.4 us (1.062)
  Pallas kernels: 80.6 us -> 85.5 us
    pallas_call x1, Pallas kernels: 80.6 us -> 85.5 us  [body(): pl.pallas_call(kernel, out_shape=(jax.ShapeDtypeStruct((OWN, D), bf16), j...]
where the time goes in v5:
time: 90.4 us; the launch traced here: 89.9 us
  Pallas kernels  85.5 us (95%)
  local copies, waits for them, and re-layouts  3.72 us (4%)
    pallas_call x1, Pallas kernels, body(): pl.pallas_call(kernel, out_shape=(jax.ShapeDtypeStruct((OWN, D), bf16), j...  85.5 us
    unnamed x7, local copies, waits for them, and re-layouts  3.72 us

profile of v5, /device:TPU:0, one launch (start us, length us, event | category | flops | bytes accessed | tf_op | source)
XLA Modules:
  0.0 89.9 jit_solution(3533675643452821204)
XLA Ops:
  0.6 85.5 %swin_backward.1 = (bf16[576,1024]{1,0:T(8,128)(2,1)}, f32[3,32,512]{2,1,0:T(8,128)}, f32[32,512]{1,0:T(8,128)}) custom-call(bf16[576,1024]{1,0:T(8,128)(2,1)} %bitcast.8, bf16[576,1024]{1,0:T(8,128)(2,1)} %bitcast.9, s32[24,1,24]{2,1,0:T(1,128)} %bitcast.11, bf16[3,1024,512]{2,1,0:T(8,128)(2,1)} %wq_h.1, bf16[512,1024]{1,0:T(8,128)(2,1)} %wo_h.1, ...), custom_call_target="tpu_custom_call" | custom-call | tf_op jit(solution)/shard_map/swin_backward/pallas_call | solution.py:458
  86.1 0.0 copy-start
  86.1 0.0 copy-start.1
  86.1 2.4 %copy.22 = bf16[24,24,1,1024]{3,1,2,0:T(8,128)(2,1)} copy(bf16[24,24,1,1024]{3,1,2,0:T(8,128)(2,1)} %bitcast.7) | data formatting | bytes 2359296
  88.5 0.0 copy-done
  88.6 0.7 copy.23
  89.2 0.0 copy-done.1
  89.2 0.6 copy.24
Async XLA Ops:
  86.1 2.4 %copy-start = (f32[3,32,512]{2,1,0:T(8,128)S(1)}, f32[3,32,512]{2,1,0:T(8,128)}, u32[]{:S(2)}) copy-start(f32[3,32,512]{2,1,0:T(8,128)} %get-tuple-element.16) | copy-start | bytes 589828
  86.1 3.1 %copy-start.1 = (f32[32,512]{1,0:T(8,128)S(1)}, f32[32,512]{1,0:T(8,128)}, u32[]{:S(2)}) copy-start(f32[32,512]{1,0:T(8,128)} %get-tuple-element.8) | copy-start | bytes 196612

commit v6 on v5

--- a/solution.py
+++ b/solution.py
@@ -128,7 +128,8 @@
         c.wait()
     out_g[...] = dot(send_m[...], g[...]).astype(bf16)
     pl.semaphore_wait(barrier, len(greeted))
-    halos[0][0].start()
+    for c in halos[0]:
+        c.start()
 
     for c in loads[2:6]:
         c.wait()
@@ -148,7 +149,8 @@
         nat[rows, :D] = (v * s).astype(bf16)
 
     out_n[...] = dot(send_m[...], nat[...]).astype(bf16)
-    halos[1][0].start()
+    for c in halos[1]:
+        c.start()
 
     def exchanges(w):
         return (
@@ -344,29 +346,27 @@
     for w in range(EARLY - 1):
         assemble(w)
     pl.loop(0, EARLY - 1)(gather)
-    for c in halos[0][1:] + halos[1][1:]:
-        c.start()
     for c in loads[6:]:
         c.wait()
     for p in range(PASSES):
         project(p, 0, EARLY - 1)
         pl.loop(0, EARLY - 1)(lambda w, p=p: attend(p, w))
     d_normed(0)
+    for i in range(3):
+        transposed(i)
     for c in halos[0][:1] + halos[1][:1]:
         c.wait_recv()
     assemble(3)
-    for i in range(3):
-        transposed(i)
     gather(jnp.int32(3))
     for p in range(PASSES):
         project(p, 3)
         attend(p, 3)
-    d_normed(2)
-    transposed(3)
     for c in halos[0][1:] + halos[1][1:]:
         c.wait_recv()
     for w in range(EARLY, WINDOWS):
         assemble(w)
+    d_normed(2)
+    transposed(3)
 
     @pl.loop(EARLY, WINDOWS)
     def _(w):

time: 90.4 us -> 83.2 us (0.920)
  Pallas kernels: 85.5 us -> 78.6 us
    pallas_call x1, Pallas kernels: 85.5 us -> 78.6 us  [body(): pl.pallas_call(kernel, out_shape=(jax.ShapeDtypeStruct((OWN, D), bf16), j...]
where the time goes in v6:
time: 83.2 us; the launch traced here: 83 us
  Pallas kernels  78.6 us (94%)
  local copies, waits for them, and re-layouts  3.72 us (4%)
    pallas_call x1, Pallas kernels, body(): pl.pallas_call(kernel, out_shape=(jax.ShapeDtypeStruct((OWN, D), bf16), j...  78.6 us
    unnamed x7, local copies, waits for them, and re-layouts  3.72 us

profile of v6, /device:TPU:0, one launch (start us, length us, event | category | flops | bytes accessed | tf_op | source)
XLA Modules:
  0.0 83.0 jit_solution(3397243090755444238)
XLA Ops:
  0.6 78.6 %swin_backward.1 = (bf16[576,1024]{1,0:T(8,128)(2,1)}, f32[3,32,512]{2,1,0:T(8,128)}, f32[32,512]{1,0:T(8,128)}) custom-call(bf16[576,1024]{1,0:T(8,128)(2,1)} %bitcast.8, bf16[576,1024]{1,0:T(8,128)(2,1)} %bitcast.9, s32[24,1,24]{2,1,0:T(1,128)} %bitcast.11, bf16[3,1024,512]{2,1,0:T(8,128)(2,1)} %wq_h.1, bf16[512,1024]{1,0:T(8,128)(2,1)} %wo_h.1, ...), custom_call_target="tpu_custom_call" | custom-call | tf_op jit(solution)/shard_map/swin_backward/pallas_call | solution.py:458
  79.3 0.0 copy-start
  79.3 0.0 copy-start.1
  79.3 2.4 %copy.22 = bf16[24,24,1,1024]{3,1,2,0:T(8,128)(2,1)} copy(bf16[24,24,1,1024]{3,1,2,0:T(8,128)(2,1)} %bitcast.7) | data formatting | bytes 2359296
  81.7 0.0 copy-done
  81.7 0.7 copy.23
  82.4 0.0 copy-done.1
  82.4 0.6 copy.24
Async XLA Ops:
  79.3 2.4 %copy-start = (f32[3,32,512]{2,1,0:T(8,128)S(1)}, f32[3,32,512]{2,1,0:T(8,128)}, u32[]{:S(2)}) copy-start(f32[3,32,512]{2,1,0:T(8,128)} %get-tuple-element.16) | copy-start | bytes 589828
  79.3 3.1 %copy-start.1 = (f32[32,512]{1,0:T(8,128)S(1)}, f32[32,512]{1,0:T(8,128)}, u32[]{:S(2)}) copy-start(f32[32,512]{1,0:T(8,128)} %get-tuple-element.8) | copy-start | bytes 196612
